TPU v7x, 512 devices: a whole 4x8x8 slice. The times are simulated.
512 devices in a mesh: dp: 32 (over z, x), aug: 16 (over y, core).
Axes of the slice: x: 4, y: 8, z: 8, core: 2. Of those that a mesh axis runs over, the one named last changes fastest.
Arguments:
- images: bfloat16 [32, 3, 256, 256], P('dp'), may hold values from -8 to 8
- offsets: int32 [32, 16, 2], P('dp'), may hold values from 0 to 32
- flip_flags: int32 [32, 16], P('dp'), may hold values from 0 to 1
- out_grads: bfloat16 [32, 16, 256, 1664], P('dp', 'aug'), may hold values from -16 to 16
- weight: float32 [978432], P('aug'), may hold values from -3 to 3
- gauss_noise: float32 [978432], P('aug'), may hold values from -6 to 6
Outputs:
- new_weight: float32 [978432], P('aug')
- clipped_mean: float32 [978432], P('aug')
- grad_norms: float32 [32], P('dp')
All inputs are finite; a program needn't handle non-finite values.
Results may differ from a plain program's by a relative error of at most 0.0003.
Values may be sent and summed in bfloat16 or wider, within the bound.
No kernel may reach another device: no remote copies, remote signals or barrier semaphores. Data moves between devices by JAX's collectives and lax.ppermute only.
A program may use at most 64 MiB of HBM per device.

v0:
```python
import math

import jax
import jax.numpy as jnp
from jax import lax
from jax.sharding import PartitionSpec as P

D = 1664
PS = 14
GRID = 16
CH = 3
PATCH = 588


def shifted(value, axis, steps):
    count = lax.axis_size(axis)
    pairs = [(source, (source + steps) % count) for source in range(count)]
    return lax.ppermute(value, axis, pairs)


def patches(picture, corner, flipped):
    anchor = jnp.zeros((), jnp.int32)
    cropped = lax.dynamic_slice(picture, (anchor, corner[0], corner[1]), (CH, GRID * PS, GRID * PS))
    cropped = jnp.where(flipped > 0, cropped[:, :, ::-1], cropped)
    blocks = cropped.reshape(CH, GRID, PS, GRID, PS).transpose(0, 2, 4, 1, 3)
    return blocks.reshape(CH * PS * PS, GRID * GRID)


def pair_terms(rows_left, grads_left, rows_right, grads_right):
    gram_rows = jnp.einsum(
        "ipt,ipu->itu", rows_left, rows_right, preferred_element_type=jnp.float32
    )
    gram_grads = jnp.einsum(
        "itd,iud->itu", grads_left, grads_right, preferred_element_type=jnp.float32
    )
    return jnp.sum(gram_rows * gram_grads, axis=(1, 2))


def per_device(images, offsets, flip_flags, out_grads, weight, gauss_noise):
    aug_count = lax.axis_size("aug")
    aug_index = lax.axis_index("aug")
    clip_bound = math.sqrt(PATCH * D)
    builder = jax.vmap(patches)
    corners = lax.dynamic_index_in_dim(offsets, aug_index, 1, keepdims=False)
    flag_row = lax.dynamic_index_in_dim(flip_flags, aug_index, 1, keepdims=False)
    patch_rows = builder(images, corners, flag_row)
    grad_rows = out_grads[:, 0]
    image_count = patch_rows.shape[0]
    pair_sum = pair_terms(patch_rows, grad_rows, patch_rows, grad_rows)
    for distance in range(1, aug_count // 2 + 1):
        multiple = 1.0 if 2 * distance == aug_count else 2.0
        their_grads, their_rows = shifted((grad_rows, patch_rows), "aug", distance)
        pair_sum = pair_sum + multiple * pair_terms(their_rows, their_grads, patch_rows, grad_rows)
    squares = lax.psum(pair_sum, "aug") / (aug_count * aug_count)
    grad_norms = jnp.sqrt(squares + 1e-06)
    factor = jnp.minimum(1.0, clip_bound / grad_norms)

    def add_image(position, running):
        rows_one = lax.dynamic_index_in_dim(patch_rows, position, 0, keepdims=False)
        grads_one = lax.dynamic_index_in_dim(grad_rows, position, 0, keepdims=False)
        weight_one = lax.dynamic_index_in_dim(factor, position, 0, keepdims=False) / aug_count
        return running + weight_one * jnp.dot(
            rows_one, grads_one, preferred_element_type=jnp.float32
        )

    zero_sum = jnp.zeros((patch_rows.shape[1], grad_rows.shape[2]), jnp.float32)
    local_sum = lax.fori_loop(0, image_count, add_image, zero_sum)
    flat_sum = local_sum.reshape(-1)
    owner_shard = lax.psum_scatter(flat_sum, "aug", scatter_dimension=0, tiled=True)
    clipped_sum = lax.psum(owner_shard, "dp")
    image_total = image_count * lax.axis_size("dp")
    clipped_mean = clipped_sum / image_total
    new_weight = weight - 0.1 * (clipped_sum / clip_bound + gauss_noise)
    return (new_weight, clipped_mean, grad_norms)


def solution(mesh):
    return jax.shard_map(
        per_device,
        mesh=mesh,
        in_specs=(
            P("dp", None, None, None),
            P("dp", None, None),
            P("dp", None),
            P("dp", "aug", None, None),
            P("aug"),
            P("aug"),
        ),
        out_specs=(P("aug"), P("aug"), P("dp")),
        check_vma=False,
    )
```

profile of v0, /device:TPU:8, one launch (start us, length us, event | category | flops | bytes accessed | tf_op | source)
XLA Modules:
  0.0 716.5 jit_solution(4171635720282326090)
XLA Ops:
  7.2 6.7 collective-permute-start.11
  18.6 1.2 constant_dynamic-slice_fusion
  19.8 2.1 reverse
  21.9 1.2 fusion.46
  23.2 2.0 broadcast_select_fusion
  25.2 4.4 reshape.168
  29.6 5.9 copy.11
  35.5 3.3 reshape.171
  38.9 2.8 collective-permute-start.10
  41.7 1.9 collective-permute-start.8
  43.6 7.2 %collective-permute-start.9 = (bf16[1,256,1664]{2,1,0:T(8,128)(2,1)S(1)}, bf16[1,256,1664]{2,1,0:T(8,128)(2,1)}, u32[]{:S(2)}, u32[]{:S(2)}) collective-permute-start(bf16[1,256,1664]{2,1,0:T(8,128)(2,1)S(1)} %bitcast.101), channel_id=1, source_target_pairs={{0,5},{1,6},{2,7},{3,8},{4,9},{5,10},{6,11},{7,12},{8,13},{9,14},{... | collective-permute-start | bytes 2555912 | tf_op jit(solution)/shard_map/ppermute | solution.py:18
  50.8 2.7 collective-permute-start.6
  53.5 3.4 reshape.169
  56.9 1.4 fusion.47
  58.3 1.0 fusion.26
  59.4 11.7 %collective-permute-done.11 = bf16[1,256,1664]{2,1,0:T(8,128)(2,1)} collective-permute-done((bf16[1,256,1664]{2,1,0:T(8,128)(2,1)}, bf16[1,256,1664]{2,1,0:T(8,128)(2,1)}, u32[]{:S(2)}, u32[]{:S(2)}) %collective-permute-start.11) | collective-permute-done | bytes 852000 | tf_op jit(solution)/shard_map/ppermute | solution.py:18
  71.1 7.2 collective-permute-start.7
  78.2 1.6 fusion.4
  79.8 12.0 %collective-permute-done.10 = bf16[1,588,256]{2,1,0:T(8,128)(2,1)} collective-permute-done((bf16[1,588,256]{2,1,0:T(8,128)(2,1)}, bf16[1,588,256]{2,1,0:T(8,128)(2,1)}, u32[]{:S(2)}, u32[]{:S(2)}) %collective-permute-start.10) | collective-permute-done | bytes 301088 | tf_op jit(solution)/shard_map/ppermute | solution.py:18
  91.8 1.9 collective-permute-start.4
  93.7 2.0 fusion.34
  95.7 54.8 %collective-permute-done.9 = bf16[1,256,1664]{2,1,0:T(8,128)(2,1)} collective-permute-done((bf16[1,256,1664]{2,1,0:T(8,128)(2,1)S(1)}, bf16[1,256,1664]{2,1,0:T(8,128)(2,1)}, u32[]{:S(2)}, u32[]{:S(2)}) %collective-permute-start.9) | collective-permute-done | bytes 852000 | tf_op jit(solution)/shard_map/ppermute | solution.py:18
  150.5 6.0 collective-permute-start.5
  156.4 1.6 fusion.6
  158.1 1.9 collective-permute-start.2
  160.0 2.0 fusion.33
  161.9 39.9 %collective-permute-done.7 = bf16[1,256,1664]{2,1,0:T(8,128)(2,1)S(1)} collective-permute-done((bf16[1,256,1664]{2,1,0:T(8,128)(2,1)S(1)}, bf16[1,256,1664]{2,1,0:T(8,128)(2,1)S(1)}, u32[]{:S(2)}, u32[]{:S(2)}) %collective-permute-start.7) | collective-permute-done | bytes 852000 | tf_op jit(solution)/shard_map/ppermute | solution.py:18
  201.9 3.8 collective-permute-start.3
  206.2 2.0 fusion.32
  208.2 29.3 %collective-permute-done.5 = bf16[1,256,1664]{2,1,0:T(8,128)(2,1)S(1)} collective-permute-done((bf16[1,256,1664]{2,1,0:T(8,128)(2,1)S(1)}, bf16[1,256,1664]{2,1,0:T(8,128)(2,1)S(1)}, u32[]{:S(2)}, u32[]{:S(2)}) %collective-permute-start.5) | collective-permute-done | bytes 852000 | tf_op jit(solution)/shard_map/ppermute | solution.py:18
  237.5 1.5 collective-permute-start.1
  239.4 4.3 collective-permute-start.12
  244.6 21.3 %collective-permute-done.3 = bf16[1,256,1664]{2,1,0:T(8,128)(2,1)S(1)} collective-permute-done((bf16[1,256,1664]{2,1,0:T(8,128)(2,1)S(1)}, bf16[1,256,1664]{2,1,0:T(8,128)(2,1)S(1)}, u32[]{:S(2)}, u32[]{:S(2)}) %collective-permute-start.3) | collective-permute-done | bytes 852000 | tf_op jit(solution)/shard_map/ppermute | solution.py:18
  265.9 1.9 collective-permute-start.13
  268.3 3.2 collective-permute-start.14
  272.4 32.4 %collective-permute-done.1 = bf16[1,256,1664]{2,1,0:T(8,128)(2,1)S(1)} collective-permute-done((bf16[1,256,1664]{2,1,0:T(8,128)(2,1)S(1)}, bf16[1,256,1664]{2,1,0:T(8,128)(2,1)S(1)}, u32[]{:S(2)}, u32[]{:S(2)}) %collective-permute-start.1) | collective-permute-done | bytes 852000 | tf_op jit(solution)/shard_map/ppermute | solution.py:18
  304.7 5.6 collective-permute-start.15
  310.8 0.9 fusion.29
  311.7 54.4 %collective-permute-done.13 = bf16[1,256,1664]{2,1,0:T(8,128)(2,1)S(1)} collective-permute-done((bf16[1,256,1664]{2,1,0:T(8,128)(2,1)S(1)}, bf16[1,256,1664]{2,1,0:T(8,128)(2,1)S(1)}, u32[]{:S(2)}, u32[]{:S(2)}) %collective-permute-start.13) | collective-permute-done | bytes 852000 | tf_op jit(solution)/shard_map/ppermute | solution.py:18
  366.6 0.9 fusion.35
  374.7 33.4 %psum.14 = f32[1]{0:T(128)} all-reduce(f32[1]{0:T(128)} %bitcast.24), channel_id=1, replica_groups=mesh['dp'=32,'aug'=16] {'aug'}, use_global_device_ids=true, to_apply=%region_9.10 | all-reduce | flops 1 | bytes 8 | tf_op jit(solution)/shard_map/psum | solution.py:54
  408.9 2.6 convolution_multiply_fusion
  411.5 4.7 reshape.188
  416.3 1.4 dynamic-slice.4
  418.3 125.9 %all-reduce.6.cloned.1.call-done = f32[978432]{0:T(1024)} async-done(((f32[978432]{0:T(1024)}), f32[978432]{0:T(1024)}) %all-reduce.6.cloned.1.call-update) | async-done | bytes 3913744
  544.3 1.8 dynamic-slice.5
  546.1 160.6 %all-reduce.4.cloned.1.call-done = f32[61152]{0:T(1024)} async-done(((f32[61152]{0:T(1024)}), f32[61152]{0:T(1024)}) %all-reduce.4.cloned.1.call-update) | async-done | bytes 244624 | tf_op jit(solution)/shard_map/psum | solution.py:70
  706.7 1.8 broadcast_multiply_fusion
  (36 shorter events, 6.3 us)
Async XLA Ops:
  7.2 6.8 copy-start
  7.2 537.1 %all-reduce.6.cloned.1.call-start = ((), (), s32[]{:S(2)}) async-start(), calls=%async_computation.1 | async-start | bytes 7831552
  7.2 63.9 %collective-permute-start.11 = (bf16[1,256,1664]{2,1,0:T(8,128)(2,1)}, bf16[1,256,1664]{2,1,0:T(8,128)(2,1)}, u32[]{:S(2)}, u32[]{:S(2)}) collective-permute-start(bf16[1,256,1664]{2,1,0:T(8,128)(2,1)} %bitcast.100), channel_id=1, source_target_pairs={{0,6},{1,7},{2,8},{3,9},{4,10},{5,11},{6,12},{7,13},{8,14},{9,15},... | collective-permute-start | bytes 2555912 | tf_op jit(solution)/shard_map/ppermute | solution.py:18
  29.6 14.0 %copy-start.1 = (bf16[1,1,256,1664]{3,2,1,0:T(8,128)(2,1)S(1)}, bf16[1,1,256,1664]{3,2,1,0:T(8,128)(2,1)}, u32[]{:S(2)}) copy-start(bf16[1,1,256,1664]{3,2,1,0:T(8,128)(2,1)} %param.9) | copy-start | bytes 2555908
  38.9 52.9 %collective-permute-start.10 = (bf16[1,588,256]{2,1,0:T(8,128)(2,1)}, bf16[1,588,256]{2,1,0:T(8,128)(2,1)}, u32[]{:S(2)}, u32[]{:S(2)}) collective-permute-start(bf16[1,588,256]{2,1,0:T(8,128)(2,1)} %reshape.171), channel_id=1, source_target_pairs={{0,6},{1,7},{2,8},{3,9},{4,10},{5,11},{6,12},{7,13},{8,14},{9,15},... | collective-permute-start | bytes 903176 | tf_op jit(solution)/shard_map/ppermute | solution.py:18
  41.7 116.4 %collective-permute-start.8 = (bf16[1,588,256]{2,1,0:T(8,128)(2,1)}, bf16[1,588,256]{2,1,0:T(8,128)(2,1)}, u32[]{:S(2)}, u32[]{:S(2)}) collective-permute-start(bf16[1,588,256]{2,1,0:T(8,128)(2,1)} %reshape.171), channel_id=1, source_target_pairs={{0,5},{1,6},{2,7},{3,8},{4,9},{5,10},{6,11},{7,12},{8,13},{9,14},{... | collective-permute-start | bytes 903176 | tf_op jit(solution)/shard_map/ppermute | solution.py:18
  43.6 106.9 %collective-permute-start.9 = (bf16[1,256,1664]{2,1,0:T(8,128)(2,1)S(1)}, bf16[1,256,1664]{2,1,0:T(8,128)(2,1)}, u32[]{:S(2)}, u32[]{:S(2)}) collective-permute-start(bf16[1,256,1664]{2,1,0:T(8,128)(2,1)S(1)} %bitcast.101), channel_id=1, source_target_pairs={{0,5},{1,6},{2,7},{3,8},{4,9},{5,10},{6,11},{7,12},{8,13},{9,14},{... | collective-permute-start | bytes 2555912 | tf_op jit(solution)/shard_map/ppermute | solution.py:18
  50.8 155.3 %collective-permute-start.6 = (bf16[1,588,256]{2,1,0:T(8,128)(2,1)}, bf16[1,588,256]{2,1,0:T(8,128)(2,1)}, u32[]{:S(2)}, u32[]{:S(2)}) collective-permute-start(bf16[1,588,256]{2,1,0:T(8,128)(2,1)} %reshape.171), channel_id=1, source_target_pairs={{0,4},{1,5},{2,6},{3,7},{4,8},{5,9},{6,10},{7,11},{8,12},{9,13},{1... | collective-permute-start | bytes 903176 | tf_op jit(solution)/shard_map/ppermute | solution.py:18
  56.9 34.9 %copy-start.3 = (bf16[1,588,256]{2,1,0:T(8,128)(2,1)S(1)}, bf16[1,588,256]{2,1,0:T(8,128)(2,1)}, u32[]{:S(2)}) copy-start(bf16[1,588,256]{2,1,0:T(8,128)(2,1)} %reshape.171) | copy-start | bytes 903172
  56.9 36.8 %copy-start.2 = (bf16[588,256]{1,0:T(8,128)(2,1)S(1)}, bf16[588,256]{1,0:T(8,128)(2,1)}, u32[]{:S(2)}) copy-start(bf16[588,256]{1,0:T(8,128)(2,1)} %reshape.169) | copy-start | bytes 903172
  71.1 130.8 %collective-permute-start.7 = (bf16[1,256,1664]{2,1,0:T(8,128)(2,1)S(1)}, bf16[1,256,1664]{2,1,0:T(8,128)(2,1)S(1)}, u32[]{:S(2)}, u32[]{:S(2)}) collective-permute-start(bf16[1,256,1664]{2,1,0:T(8,128)(2,1)S(1)} %bitcast.102), channel_id=1, source_target_pairs={{0,4},{1,5},{2,6},{3,7},{4,8},{5,9},{6,10},{7,11},{8,12},{9,13},{1... | collective-permute-start | bytes 2555912 | tf_op jit(solution)/shard_map/ppermute | solution.py:18
  91.8 147.6 %collective-permute-start.4 = (bf16[1,588,256]{2,1,0:T(8,128)(2,1)S(1)}, bf16[1,588,256]{2,1,0:T(8,128)(2,1)S(1)}, u32[]{:S(2)}, u32[]{:S(2)}) collective-permute-start(bf16[1,588,256]{2,1,0:T(8,128)(2,1)S(1)} %copy-done.3), channel_id=1, source_target_pairs={{0,3},{1,4},{2,5},{3,6},{4,7},{5,8},{6,9},{7,10},{8,11},{9,12},{10... | collective-permute-start | bytes 903176 | tf_op jit(solution)/shard_map/ppermute | solution.py:18
  150.5 87.0 %collective-permute-start.5 = (bf16[1,256,1664]{2,1,0:T(8,128)(2,1)S(1)}, bf16[1,256,1664]{2,1,0:T(8,128)(2,1)S(1)}, u32[]{:S(2)}, u32[]{:S(2)}) collective-permute-start(bf16[1,256,1664]{2,1,0:T(8,128)(2,1)S(1)} %bitcast.103), channel_id=1, source_target_pairs={{0,3},{1,4},{2,5},{3,6},{4,7},{5,8},{6,9},{7,10},{8,11},{9,12},{10... | collective-permute-start | bytes 2555912 | tf_op jit(solution)/shard_map/ppermute | solution.py:18
  158.1 110.2 %collective-permute-start.2 = (bf16[1,588,256]{2,1,0:T(8,128)(2,1)S(1)}, bf16[1,588,256]{2,1,0:T(8,128)(2,1)S(1)}, u32[]{:S(2)}, u32[]{:S(2)}) collective-permute-start(bf16[1,588,256]{2,1,0:T(8,128)(2,1)S(1)} %copy-done.3), channel_id=1, source_target_pairs={{0,2},{1,3},{2,4},{3,5},{4,6},{5,7},{6,8},{7,9},{8,10},{9,11},{10,... | collective-permute-start | bytes 903176 | tf_op jit(solution)/shard_map/ppermute | solution.py:18
  201.9 64.0 %collective-permute-start.3 = (bf16[1,256,1664]{2,1,0:T(8,128)(2,1)S(1)}, bf16[1,256,1664]{2,1,0:T(8,128)(2,1)S(1)}, u32[]{:S(2)}, u32[]{:S(2)}) collective-permute-start(bf16[1,256,1664]{2,1,0:T(8,128)(2,1)S(1)} %bitcast.104), channel_id=1, source_target_pairs={{0,2},{1,3},{2,4},{3,5},{4,6},{5,7},{6,8},{7,9},{8,10},{9,11},{10,... | collective-permute-start | bytes 2555912 | tf_op jit(solution)/shard_map/ppermute | solution.py:18
  206.2 104.6 %collective-permute-start = (bf16[1,588,256]{2,1,0:T(8,128)(2,1)S(1)}, bf16[1,588,256]{2,1,0:T(8,128)(2,1)S(1)}, u32[]{:S(2)}, u32[]{:S(2)}) collective-permute-start(bf16[1,588,256]{2,1,0:T(8,128)(2,1)S(1)} %copy-done.3), channel_id=1, source_target_pairs={{0,1},{1,2},{2,3},{3,4},{4,5},{5,6},{6,7},{7,8},{8,9},{9,10},{10,1... | collective-permute-start | bytes 903176 | tf_op jit(solution)/shard_map/ppermute | solution.py:18
  237.5 67.3 %collective-permute-start.1 = (bf16[1,256,1664]{2,1,0:T(8,128)(2,1)S(1)}, bf16[1,256,1664]{2,1,0:T(8,128)(2,1)S(1)}, u32[]{:S(2)}, u32[]{:S(2)}) collective-permute-start(bf16[1,256,1664]{2,1,0:T(8,128)(2,1)S(1)} %bitcast.105), channel_id=1, source_target_pairs={{0,1},{1,2},{2,3},{3,4},{4,5},{5,6},{6,7},{7,8},{8,9},{9,10},{10,1... | collective-permute-start | bytes 2555912 | tf_op jit(solution)/shard_map/ppermute | solution.py:18
  239.4 127.2 %collective-permute-start.12 = (bf16[1,588,256]{2,1,0:T(8,128)(2,1)S(1)}, bf16[1,588,256]{2,1,0:T(8,128)(2,1)S(1)}, u32[]{:S(2)}, u32[]{:S(2)}) collective-permute-start(bf16[1,588,256]{2,1,0:T(8,128)(2,1)S(1)} %copy-done.3), channel_id=1, source_target_pairs={{0,7},{1,8},{2,9},{3,10},{4,11},{5,12},{6,13},{7,14},{8,15},{9,0},... | collective-permute-start | bytes 903176 | tf_op jit(solution)/shard_map/ppermute | solution.py:18
  265.9 100.3 %collective-permute-start.13 = (bf16[1,256,1664]{2,1,0:T(8,128)(2,1)S(1)}, bf16[1,256,1664]{2,1,0:T(8,128)(2,1)S(1)}, u32[]{:S(2)}, u32[]{:S(2)}) collective-permute-start(bf16[1,256,1664]{2,1,0:T(8,128)(2,1)S(1)} %bitcast.106), channel_id=1, source_target_pairs={{0,7},{1,8},{2,9},{3,10},{4,11},{5,12},{6,13},{7,14},{8,15},{9,0},... | collective-permute-start | bytes 2555912 | tf_op jit(solution)/shard_map/ppermute | solution.py:18
  268.3 104.9 %collective-permute-start.14 = (bf16[1,588,256]{2,1,0:T(8,128)(2,1)S(1)}, bf16[1,588,256]{2,1,0:T(8,128)(2,1)S(1)}, u32[]{:S(2)}, u32[]{:S(2)}) collective-permute-start(bf16[1,588,256]{2,1,0:T(8,128)(2,1)S(1)} %copy-done.3), channel_id=1, source_target_pairs={{0,8},{1,9},{2,10},{3,11},{4,12},{5,13},{6,14},{7,15},{8,0},{9,1},... | collective-permute-start | bytes 903176 | tf_op jit(solution)/shard_map/ppermute | solution.py:18
  304.7 67.9 %collective-permute-start.15 = (bf16[1,256,1664]{2,1,0:T(8,128)(2,1)S(1)}, bf16[1,256,1664]{2,1,0:T(8,128)(2,1)S(1)}, u32[]{:S(2)}, u32[]{:S(2)}) collective-permute-start(bf16[1,256,1664]{2,1,0:T(8,128)(2,1)S(1)} %bitcast.107), channel_id=1, source_target_pairs={{0,8},{1,9},{2,10},{3,11},{4,12},{5,13},{6,14},{7,15},{8,0},{9,1},... | collective-permute-start | bytes 2555912 | tf_op jit(solution)/shard_map/ppermute | solution.py:18
  416.2 290.5 %copy-start.4 = (f32[61152]{0:T(1024)S(1)}, f32[61152]{0:T(1024)}, u32[]{:S(2)}) copy-start(f32[61152]{0:T(1024)} %param.10) | copy-start | bytes 733828
  416.2 290.5 %copy-start.5 = (f32[61152]{0:T(1024)S(1)}, f32[61152]{0:T(1024)}, u32[]{:S(2)}) copy-start(f32[61152]{0:T(1024)} %param.11) | copy-start | bytes 733828
  416.2 290.5 %all-reduce.4.cloned.1.call-start = ((), (), s32[]{:S(2)}) async-start(), calls=%async_computation | async-start | bytes 491520 | tf_op jit(solution)/shard_map/psum | solution.py:70
Sparse Core Ops, SparseCore 0:
  416.3 127.8 all-reduce.5
  548.7 157.9 all-reduce.3
where the time goes:
time: 718 us; the launch traced here: 716 us
  waiting for transfers between devices  542 us (75%)
  starting transfers between devices  58.7 us (8%)
  blocking collectives  33.4 us (5%)
  local copies, waits for them, and re-layouts  28.9 us (4%)
  between operations  26.6 us (4%)
  matrix products  21.4 us (3%)
    ppermute x16, waiting for transfers between devices, shifted(): return lax.ppermute(value, axis, pairs)  256 us
    psum x1, waiting for transfers between devices, per_device(): clipped_sum = lax.psum(owner_shard, 'dp')  161 us
    unnamed x3, waiting for transfers between devices  126 us
    ppermute x16, starting transfers between devices, shifted(): return lax.ppermute(value, axis, pairs)  58.6 us
    psum x1, blocking collectives, per_device(): squares = lax.psum(pair_sum, 'aug') / (aug_count * aug_count)  33.4 us
  transfers between devices with their start and end apart: 18, of which 10 were waited for; matrix products, arithmetic and copies ran while one was open for 6% of the time, Pallas kernels for 0%

commit v1 on v0

v1 whole, which is shorter than its diff:
```python
import functools
import math

import jax
import jax.numpy as jnp
from jax import lax
from jax.experimental import pallas as pl
from jax.experimental.pallas import tpu as pltpu
from jax.sharding import PartitionSpec as P

D = 1664
PS = 14
GRID = 16
CH = 3
SIDE = 256
PATCH = 588
AUG = 16
LANES = 128
BLOCKS = D // LANES
CLIP = math.sqrt(PATCH * D)
SHARD = PATCH * D // AUG
SROWS = 38
MROWS = 40
ROWS = 512
SPARE = 8
PITCH = SIDE + SPARE


def gradient_kernel(offs, flags, img, grads, msg, sel, cols, pat, gord, flat):
    lane = lax.broadcasted_iota(jnp.int32, (SIDE, SIDE), 1)
    row = lax.broadcasted_iota(jnp.int32, (SIDE, SIDE), 0)
    slot = lane // 16
    xpos = (lane % 16) * PS
    for k in range(AUG):
        pixel = xpos + ((slot + (16 - k)) % 16)
        corner = offs[k, 1]
        flipped = flags[k]
        first = jnp.where(flipped > 0, corner + (GRID * PS - 1), corner)
        sign = jnp.where(flipped > 0, -1, 1)
        hit = row == first + sign * pixel
        sel[:, k * SIDE:(k + 1) * SIDE] = jnp.where(hit, 1.0, 0.0).astype(jnp.bfloat16)

    for c in range(CH):
        for k in range(AUG):
            picked = jnp.dot(
                img[c], sel[:, k * SIDE:(k + 1) * SIDE], preferred_element_type=jnp.float32
            )
            for h in range(2):
                cols[c, 2 * k + h, 0:SIDE, :] = picked[:, h * LANES:(h + 1) * LANES]

    slots = lax.broadcasted_iota(jnp.int32, (8, LANES), 1) // 16
    masks = [slots == s for s in range(8)]

    def assemble(step, carry):
        c = step // GRID
        y = step % GRID
        for half in range(2):
            parts = []
            for k in range(AUG):
                start = offs[k, 0] + PS * y + 8 * half
                parts.append([cols[c, 2 * k + h, pl.ds(start, 8), :] for h in range(2)])
            for v in range(PS):
                pair = []
                for h in range(2):
                    value = None
                    for s in range(8):
                        k = (8 * h + s - v) % 16
                        piece = parts[k][h]
                        value = piece if value is None else jnp.where(masks[s], piece, value)
                    pair.append(value)
                shift = 16 * v
                turn = shift % LANES
                if turn:
                    low = pltpu.roll(pair[0], LANES - turn, 1)
                    high = pltpu.roll(pair[1], LANES - turn, 1)
                    keep = slots < (LANES - turn) // 16
                    pair = [jnp.where(keep, low, high), jnp.where(keep, high, low)]
                if shift >= LANES:
                    pair = pair[::-1]
                whole = jnp.concatenate(pair, axis=1)
                pat[half, v, c, :, pl.ds(pl.multiple_of(y * SIDE, SIDE), SIDE)] = whole
        return carry

    lax.fori_loop(0, CH * GRID, assemble, 0)

    for y in range(GRID):
        for k in range(AUG):
            gord[(y * AUG + k) * 16:(y * AUG + k + 1) * 16, :] = grads[k, y * 16:(y + 1) * 16, :]
    for half in range(2):
        taken = 8 if half == 0 else PS - 8
        for v in range(PS):
            left = pat[half, v].reshape(CH * 8, AUG * SIDE).astype(jnp.bfloat16)
            total = jnp.dot(left, gord[...], preferred_element_type=jnp.float32)
            for c in range(CH):
                first = c * PS * PS + half * 8 * PS + v
                flat[pl.ds(first, taken, stride=PS), :] = total[c * 8:c * 8 + taken, :]

    flat[PATCH:, :] = jnp.zeros((4, LANES), jnp.float32)
    values = flat[...]
    squares = jnp.sum(values * values)
    for b in range(AUG):
        first = 147 * b // 4
        msg[b, 0:SROWS, :] = flat[first:first + SROWS, :]
        msg[b, SROWS:MROWS, :] = jnp.full((MROWS - SROWS, LANES), squares, jnp.float32)


def shard_kernel(index, parts, term, norm, lined):
    squares = jnp.zeros((1, LANES), jnp.float32)
    for a in range(AUG):
        squares = squares + parts[a, SROWS:SROWS + 1, :]
    length = jnp.sqrt(squares / (AUG * AUG) + 1e-6)
    norm[...] = jnp.broadcast_to(length, (8, LANES))
    scale = jnp.minimum(1.0, CLIP / length) / AUG
    for a in range(BLOCKS):
        lined[pl.ds(a, SROWS, stride=BLOCKS), :] = parts[a, 0:SROWS, :] * scale
    lined[SROWS * BLOCKS:, :] = jnp.zeros((lined.shape[0] - SROWS * BLOCKS, LANES), jnp.float32)
    ahead = (index[0] * (SHARD % D)) % D
    rows = ahead // LANES
    lanes = ahead % LANES
    near = lined[pl.ds(rows, ROWS), :]
    far = lined[pl.ds(rows + 1, ROWS), :]
    lane = lax.broadcasted_iota(jnp.int32, (ROWS, LANES), 1)
    mixed = jnp.where(lane >= lanes, near, far)
    term[...] = pltpu.roll(mixed, (LANES - lanes) % LANES, 1)


VMEM = pl.BlockSpec(memory_space=pltpu.VMEM)
SMEM = pl.BlockSpec(memory_space=pltpu.SMEM)


def per_device(images, offsets, flip_flags, out_grads, weight, gauss_noise):
    aug_index = lax.axis_index("aug")
    images_in_all = lax.axis_size("dp")
    wide = jnp.pad(out_grads[0, 0], ((0, 0), (0, AUG * LANES - D)))
    blocks = wide.reshape(GRID * GRID, AUG, LANES).transpose(1, 0, 2)
    blocks = lax.all_to_all(blocks, "aug", 0, 0)
    parts = pl.pallas_call(
        gradient_kernel,
        out_shape=jax.ShapeDtypeStruct((AUG, MROWS, LANES), jnp.float32),
        in_specs=[SMEM, SMEM, VMEM, VMEM],
        out_specs=VMEM,
        scratch_shapes=[
            pltpu.VMEM((SIDE, AUG * SIDE), jnp.bfloat16),
            pltpu.VMEM((CH, 2 * AUG, PITCH, LANES), jnp.float32),
            pltpu.VMEM((2, PS, CH, 8, AUG * SIDE), jnp.float32),
            pltpu.VMEM((AUG * SIDE, LANES), jnp.bfloat16),
            pltpu.VMEM((PATCH + 4, LANES), jnp.float32),
        ],
        compiler_params=pltpu.CompilerParams(vmem_limit_bytes=52 * 1024 * 1024),
    )(offsets[0], flip_flags[0], images[0], blocks)
    parts = lax.all_to_all(parts, "aug", 0, 0)
    term, norm = pl.pallas_call(
        shard_kernel,
        out_shape=(
            jax.ShapeDtypeStruct((ROWS, LANES), jnp.float32),
            jax.ShapeDtypeStruct((8, LANES), jnp.float32),
        ),
        in_specs=[SMEM, VMEM],
        out_specs=(VMEM, VMEM),
        scratch_shapes=[pltpu.VMEM((ROWS + 16, LANES), jnp.float32)],
    )(aug_index.reshape(1), parts)
    pieces = lax.all_to_all(term.reshape(images_in_all, -1, LANES), "dp", 0, 0)
    piece = jnp.sum(pieces, axis=0)
    spread = jnp.broadcast_to(piece[None], pieces.shape)
    clipped_sum = lax.all_to_all(spread, "dp", 0, 0).reshape(-1)[:SHARD]
    clipped_mean = clipped_sum / images_in_all
    new_weight = weight - 0.1 * (clipped_sum / CLIP + gauss_noise)
    return (new_weight, clipped_mean, norm[0, 0:1])


def solution(mesh):
    return jax.shard_map(
        per_device,
        mesh=mesh,
        in_specs=(
            P("dp", None, None, None),
            P("dp", None, None),
            P("dp", None),
            P("dp", "aug", None, None),
            P("aug"),
            P("aug"),
        ),
        out_specs=(P("aug"), P("aug"), P("dp")),
        check_vma=False,
    )
```

time: 718 us -> 123 us (0.17)
  the two profiles are of different devices: /device:TPU:8 before, /device:TPU:1 now
where the time goes in v1:
time: 123 us; the launch traced here: 122 us
  waiting for transfers between devices  50.2 us (41%)
  blocking collectives  24.1 us (20%)
  Pallas kernels  21.5 us (17%)
  starting transfers between devices  18 us (15%)
  local copies, waits for them, and re-layouts  6.97 us (6%)
    all_to_all x1, waiting for transfers between devices, per_device(): blocks = lax.all_to_all(blocks, 'aug', 0, 0)  27.2 us
    all_to_all x1, blocking collectives, per_device(): pieces = lax.all_to_all(term.reshape(images_in_all, -1, LANES), 'dp', 0, 0)  24.1 us
    pallas_call x1, Pallas kernels, per_device(): pl.pallas_call(gradient_kernel, out_shape=jax.ShapeDtypeStruct((AUG, MROW...  19.6 us
    all_to_all x1, waiting for transfers between devices, per_device(): parts = lax.all_to_all(parts, 'aug', 0, 0)  13.1 us
    all_to_all x1, starting transfers between devices, per_device(): blocks = lax.all_to_all(blocks, 'aug', 0, 0)  10.5 us
    all_to_all x1, waiting for transfers between devices, per_device(): clipped_sum = lax.all_to_all(spread, 'dp', 0, 0).reshape(-1)[:SHARD]  9.96 us
    all_to_all x1, starting transfers between devices, per_device(): clipped_sum = lax.all_to_all(spread, 'dp', 0, 0).reshape(-1)[:SHARD]  4 us
    unnamed x13, local copies, waits for them, and re-layouts  3.6 us
  transfers between devices with their start and end apart: 3, of which 3 were waited for; matrix products, arithmetic and copies ran while one was open for 1% of the time, Pallas kernels for 0%

profile of v1, /device:TPU:1, one launch (start us, length us, event | category | flops | bytes accessed | tf_op | source)
XLA Modules:
  0.0 122.3 jit_solution(2877081496977332448)
XLA Ops:
  0.6 1.5 %copy.10 = bf16[1,1,256,1664]{2,3,1,0:T(8,128)(2,1)S(1)} copy(bf16[1,1,256,1664]{3,2,1,0:T(8,128)(2,1)} %param.9) | data formatting | bytes 1703936 | tf_op args[3]
  2.2 0.1 pad.4
  2.3 1.3 %copy.11 = bf16[256,16,128]{2,0,1:T(8,128)(2,1)} copy(bf16[256,16,128]{0,2,1:T(8,128)(2,1)S(1)} %bitcast.12) | data formatting | bytes 2097152 | tf_op jit(solution)/shard_map/reshape | solution.py:135
  3.6 0.0 copy-start
  3.6 10.5 %all-to-all-start = ((bf16[16,256,128]{2,1,0:T(8,128)(2,1)}), bf16[16,256,128]{2,1,0:T(8,128)(2,1)S(1)}, u32[]{:S(2)}, u32[]{:S(2)}) async-start(bf16[16,256,128]{2,1,0:T(8,128)(2,1)} %bitcast.6), calls=%async_computation | async-start | bytes 2097152 | tf_op jit(solution)/shard_map/all_to_all | solution.py:136
  14.0 0.0 copy-start.5
  14.0 0.7 copy-done.5
  14.7 0.1 copy.12.offs
  14.8 27.2 %all-to-all-done.grads = bf16[16,256,128]{2,1,0:T(8,128)(2,1)S(1)} async-done(((bf16[16,256,128]{2,1,0:T(8,128)(2,1)}), bf16[16,256,128]{2,1,0:T(8,128)(2,1)S(1)}, u32[]{:S(2)}, u32[]{:S(2)}) %all-to-all-start) | async-done | bytes 1048608 | tf_op jit(solution)/shard_map/all_to_all | solution.py:136
  42.0 0.0 copy-start.1
  42.0 0.0 copy-done
  42.0 0.7 copy-done.1
  42.6 19.6 %shard_map.85 = f32[16,40,128]{2,1,0:T(8,128)} custom-call(s32[16,2]{1,0:T(8,128)S(1)} %copy.12.offs, s32[16]{0:T(128)S(1)} %bitcast.11, bf16[3,256,256]{2,1,0:T(8,128)(2,1)S(1)} %bitcast.10, bf16[16,256,128]{2,1,0:T(8,128)(2,1)S(1)} %all-to-all-done.grads), custom_call_target="tpu_custom_call" | custom-call | tf_op jit(solution)/shard_map/pallas_call | solution.py:137
  62.2 3.5 %all-to-all-start.1 = ((f32[16,40,128]{2,1,0:T(8,128)}), f32[16,40,128]{2,1,0:T(8,128)S(1)}, u32[]{:S(2)}, u32[]{:S(2)}) async-start(f32[16,40,128]{2,1,0:T(8,128)} %shard_map.85), calls=%async_computation.1 | async-start | bytes 655360 | tf_op jit(solution)/shard_map/all_to_all | solution.py:151
  65.8 13.1 %all-to-all-done.1.parts = f32[16,40,128]{2,1,0:T(8,128)S(1)} async-done(((f32[16,40,128]{2,1,0:T(8,128)}), f32[16,40,128]{2,1,0:T(8,128)S(1)}, u32[]{:S(2)}, u32[]{:S(2)}) %all-to-all-start.1) | async-done | bytes 327712 | tf_op jit(solution)/shard_map/all_to_all | solution.py:151
  78.8 0.0 copy-start.2
  78.8 0.7 copy-done.2
  79.6 1.9 %shard_map.86 = (f32[512,128]{1,0:T(8,128)}, f32[8,128]{1,0:T(8,128)}) custom-call(s32[1]{0:T(128)} %bitcast.index, f32[16,40,128]{2,1,0:T(8,128)} %copy-done.2), custom_call_target="tpu_custom_call" | custom-call | tf_op jit(solution)/shard_map/pallas_call | solution.py:152
  81.4 24.1 %all_to_all.20 = f32[32,16,128]{2,1,0:T(8,128)S(1)} all-to-all(f32[32,16,128]{2,1,0:T(8,128)} %bitcast.15), channel_id=1, replica_groups=mesh['dp'=32,'aug'=16] {'dp'}, dimensions={0} | all-to-all | bytes 524288 | tf_op jit(solution)/shard_map/all_to_all | solution.py:162
  105.6 0.7 broadcast_in_dim.2
  106.3 0.0 copy-start.3
  106.3 0.0 copy-start.4
  106.3 4.0 %all-to-all-start.3 = ((f32[32,16,128]{2,1,0:T(8,128)}), f32[32,16,128]{2,1,0:T(8,128)S(1)}, u32[]{:S(2)}, u32[]{:S(2)}) async-start(f32[32,16,128]{2,1,0:T(8,128)} %broadcast_in_dim.2), calls=%async_computation.3 | async-start | bytes 524288 | tf_op jit(solution)/shard_map/all_to_all | solution.py:165
  110.3 1.2 slice.7
  111.5 10.0 %all-to-all-done.3 = f32[32,16,128]{2,1,0:T(8,128)S(1)} async-done(((f32[32,16,128]{2,1,0:T(8,128)}), f32[32,16,128]{2,1,0:T(8,128)S(1)}, u32[]{:S(2)}, u32[]{:S(2)}) %all-to-all-start.3) | async-done | bytes 262176 | tf_op jit(solution)/shard_map/all_to_all | solution.py:165
  121.5 0.0 copy-done.3
  121.5 0.0 copy-done.4
  121.5 0.8 slice_multiply_fusion
  (1 shorter events, 0.0 us)
Async XLA Ops:
  3.6 38.4 %copy-start = (bf16[1,3,256,256]{3,2,1,0:T(8,128)(2,1)S(1)}, bf16[1,3,256,256]{3,2,1,0:T(8,128)(2,1)}, u32[]{:S(2)}) copy-start(bf16[1,3,256,256]{3,2,1,0:T(8,128)(2,1)} %param.6) | copy-start | bytes 1179652
  3.6 38.4 %all-to-all-start = ((bf16[16,256,128]{2,1,0:T(8,128)(2,1)}), bf16[16,256,128]{2,1,0:T(8,128)(2,1)S(1)}, u32[]{:S(2)}, u32[]{:S(2)}) async-start(bf16[16,256,128]{2,1,0:T(8,128)(2,1)} %bitcast.6), calls=%async_computation | async-start | bytes 2097152 | tf_op jit(solution)/shard_map/all_to_all | solution.py:136
  14.0 0.7 copy-start.5
  42.0 0.7 copy-start.1
  62.2 16.6 %all-to-all-start.1 = ((f32[16,40,128]{2,1,0:T(8,128)}), f32[16,40,128]{2,1,0:T(8,128)S(1)}, u32[]{:S(2)}, u32[]{:S(2)}) async-start(f32[16,40,128]{2,1,0:T(8,128)} %shard_map.85), calls=%async_computation.1 | async-start | bytes 655360 | tf_op jit(solution)/shard_map/all_to_all | solution.py:151
  78.8 0.7 copy-start.2
  106.3 15.2 %copy-start.3 = (f32[61152]{0:T(1024)S(1)}, f32[61152]{0:T(1024)}, u32[]{:S(2)}) copy-start(f32[61152]{0:T(1024)} %param.10) | copy-start | bytes 733828
  106.3 15.2 %copy-start.4 = (f32[61152]{0:T(1024)S(1)}, f32[61152]{0:T(1024)}, u32[]{:S(2)}) copy-start(f32[61152]{0:T(1024)} %param.11) | copy-start | bytes 733828
  106.3 15.2 %all-to-all-start.3 = ((f32[32,16,128]{2,1,0:T(8,128)}), f32[32,16,128]{2,1,0:T(8,128)S(1)}, u32[]{:S(2)}, u32[]{:S(2)}) async-start(f32[32,16,128]{2,1,0:T(8,128)} %broadcast_in_dim.2), calls=%async_computation.3 | async-start | bytes 524288 | tf_op jit(solution)/shard_map/all_to_all | solution.py:165

commit v2 on v1

--- a/solution.py
+++ b/solution.py
@@ -17,16 +17,18 @@
 AUG = 16
 LANES = 128
 BLOCKS = D // LANES
+COLS = D // AUG
 CLIP = math.sqrt(PATCH * D)
 SHARD = PATCH * D // AUG
 SROWS = 38
 MROWS = 40
 ROWS = 512
 SPARE = 8
+MIB = 1024 * 1024
 PITCH = SIDE + SPARE
 
 
-def gradient_kernel(offs, flags, img, grads, msg, sel, cols, pat, gord, flat):
+def patch_kernel(offs, flags, img, pat, sel, cols, held):
     lane = lax.broadcasted_iota(jnp.int32, (SIDE, SIDE), 1)
     row = lax.broadcasted_iota(jnp.int32, (SIDE, SIDE), 0)
     slot = lane // 16
@@ -47,6 +49,7 @@
             )
             for h in range(2):
                 cols[c, 2 * k + h, 0:SIDE, :] = picked[:, h * LANES:(h + 1) * LANES]
+            cols[c, 2 * k:2 * k + 2, SIDE:, :] = jnp.zeros((2, SPARE, LANES), jnp.float32)
 
     slots = lax.broadcasted_iota(jnp.int32, (8, LANES), 1) // 16
     masks = [slots == s for s in range(8)]
@@ -77,30 +80,37 @@
                     pair = [jnp.where(keep, low, high), jnp.where(keep, high, low)]
                 if shift >= LANES:
                     pair = pair[::-1]
-                whole = jnp.concatenate(pair, axis=1)
-                pat[half, v, c, :, pl.ds(pl.multiple_of(y * SIDE, SIDE), SIDE)] = whole
+                for h in range(2):
+                    held[v, 8 * half:8 * half + 8, h * LANES:(h + 1) * LANES] = pair[h]
+        for v in range(PS):
+            place = pl.ds(pl.multiple_of(y * SIDE, SIDE), SIDE)
+            pat[v, c, :, place] = held[v].astype(jnp.bfloat16)
         return carry
 
     lax.fori_loop(0, CH * GRID, assemble, 0)
 
-    for y in range(GRID):
-        for k in range(AUG):
-            gord[(y * AUG + k) * 16:(y * AUG + k + 1) * 16, :] = grads[k, y * 16:(y + 1) * 16, :]
-    for half in range(2):
-        taken = 8 if half == 0 else PS - 8
-        for v in range(PS):
-            left = pat[half, v].reshape(CH * 8, AUG * SIDE).astype(jnp.bfloat16)
-            total = jnp.dot(left, gord[...], preferred_element_type=jnp.float32)
-            for c in range(CH):
-                first = c * PS * PS + half * 8 * PS + v
-                flat[pl.ds(first, taken, stride=PS), :] = total[c * 8:c * 8 + taken, :]
-
-    flat[PATCH:, :] = jnp.zeros((4, LANES), jnp.float32)
-    values = flat[...]
+
+def gradient_kernel(pat, grads, msg, near, gord, flat, sem):
+    fetch = pltpu.make_async_copy(pat, near, sem)
+    fetch.start()
+    for k in range(AUG):
+        turned = grads[k].T
+        for y in range(GRID):
+            gord[(y * AUG + k) * 16:(y * AUG + k + 1) * 16, :] = turned[y * 16:(y + 1) * 16, :]
+    fetch.wait()
+    left = near[...].reshape(PS * CH * 16, AUG * SIDE)
+    total = jnp.dot(left, gord[...], preferred_element_type=jnp.float32)
+    for v in range(PS):
+        for c in range(CH):
+            first = v * CH * 16 + c * 16
+            flat[pl.ds(c * PS * PS + v, PS, stride=PS), 0:COLS] = total[first:first + PS, :]
+
+    flat[PATCH:, 0:COLS] = jnp.zeros((4, COLS), jnp.float32)
+    values = flat[:, 0:COLS]
     squares = jnp.sum(values * values)
     for b in range(AUG):
         first = 147 * b // 4
-        msg[b, 0:SROWS, :] = flat[first:first + SROWS, :]
+        msg[b, 0:SROWS, 0:COLS] = flat[first:first + SROWS, 0:COLS]
         msg[b, SROWS:MROWS, :] = jnp.full((MROWS - SROWS, LANES), squares, jnp.float32)
 
 
@@ -111,8 +121,14 @@
     length = jnp.sqrt(squares / (AUG * AUG) + 1e-6)
     norm[...] = jnp.broadcast_to(length, (8, LANES))
     scale = jnp.minimum(1.0, CLIP / length) / AUG
-    for a in range(BLOCKS):
-        lined[pl.ds(a, SROWS, stride=BLOCKS), :] = parts[a, 0:SROWS, :] * scale
+    lane = lax.broadcasted_iota(jnp.int32, (SROWS, LANES), 1)
+    for block in range(BLOCKS):
+        value = None
+        for a in range(LANES * block // COLS, (LANES * block + LANES - 1) // COLS + 1):
+            begin = a * COLS - LANES * block
+            piece = pltpu.roll(parts[a, 0:SROWS, :], begin % LANES, 1) * scale
+            value = piece if value is None else jnp.where(lane >= begin, piece, value)
+        lined[pl.ds(block, SROWS, stride=BLOCKS), :] = value
     lined[SROWS * BLOCKS:, :] = jnp.zeros((lined.shape[0] - SROWS * BLOCKS, LANES), jnp.float32)
     ahead = (index[0] * (SHARD % D)) % D
     rows = ahead // LANES
@@ -131,23 +147,36 @@
 def per_device(images, offsets, flip_flags, out_grads, weight, gauss_noise):
     aug_index = lax.axis_index("aug")
     images_in_all = lax.axis_size("dp")
-    wide = jnp.pad(out_grads[0, 0], ((0, 0), (0, AUG * LANES - D)))
-    blocks = wide.reshape(GRID * GRID, AUG, LANES).transpose(1, 0, 2)
+    blocks = out_grads[0, 0].T.reshape(AUG, COLS, GRID * GRID)
     blocks = lax.all_to_all(blocks, "aug", 0, 0)
-    parts = pl.pallas_call(
-        gradient_kernel,
-        out_shape=jax.ShapeDtypeStruct((AUG, MROWS, LANES), jnp.float32),
-        in_specs=[SMEM, SMEM, VMEM, VMEM],
+    pat = pl.pallas_call(
+        patch_kernel,
+        out_shape=jax.ShapeDtypeStruct((PS, CH, 16, AUG * SIDE), jnp.bfloat16),
+        in_specs=[SMEM, SMEM, VMEM],
         out_specs=VMEM,
         scratch_shapes=[
             pltpu.VMEM((SIDE, AUG * SIDE), jnp.bfloat16),
             pltpu.VMEM((CH, 2 * AUG, PITCH, LANES), jnp.float32),
-            pltpu.VMEM((2, PS, CH, 8, AUG * SIDE), jnp.float32),
-            pltpu.VMEM((AUG * SIDE, LANES), jnp.bfloat16),
+            pltpu.VMEM((PS, 16, SIDE), jnp.float32),
+        ],
+        compiler_params=pltpu.CompilerParams(vmem_limit_bytes=28 * MIB),
+        cost_estimate=pl.CostEstimate(
+            flops=20_000_000_000, bytes_accessed=20_000_000, transcendentals=0
+        ),
+    )(offsets[0], flip_flags[0], images[0])
+    parts = pl.pallas_call(
+        gradient_kernel,
+        out_shape=jax.ShapeDtypeStruct((AUG, MROWS, LANES), jnp.float32),
+        in_specs=[pl.BlockSpec(memory_space=pl.ANY), VMEM],
+        out_specs=VMEM,
+        scratch_shapes=[
+            pltpu.VMEM((PS, CH, 16, AUG * SIDE), jnp.bfloat16),
+            pltpu.VMEM((AUG * SIDE, COLS), jnp.bfloat16),
             pltpu.VMEM((PATCH + 4, LANES), jnp.float32),
+            pltpu.SemaphoreType.DMA,
         ],
-        compiler_params=pltpu.CompilerParams(vmem_limit_bytes=52 * 1024 * 1024),
-    )(offsets[0], flip_flags[0], images[0], blocks)
+        compiler_params=pltpu.CompilerParams(vmem_limit_bytes=48 * MIB),
+    )(pat, blocks)
     parts = lax.all_to_all(parts, "aug", 0, 0)
     term, norm = pl.pallas_call(
         shard_kernel,
@@ -158,6 +187,7 @@
         in_specs=[SMEM, VMEM],
         out_specs=(VMEM, VMEM),
         scratch_shapes=[pltpu.VMEM((ROWS + 16, LANES), jnp.float32)],
+        compiler_params=pltpu.CompilerParams(vmem_limit_bytes=8 * MIB),
     )(aug_index.reshape(1), parts)
     pieces = lax.all_to_all(term.reshape(images_in_all, -1, LANES), "dp", 0, 0)
     piece = jnp.sum(pieces, axis=0)

time: 123 us -> 100 us (0.81)
  waiting for transfers between devices: 50.2 us -> 27.5 us
  local copies, waits for them, and re-layouts: 6.97 us -> 8.3 us
    all_to_all x1, waiting for transfers between devices: 27.2 us -> 3.96 us  [per_device(): blocks = lax.all_to_all(blocks, 'aug', 0, 0)]
    pallas_call x0 -> x1, Pallas kernels: none -> 15.2 us  [per_device(): pl.pallas_call(patch_kernel, out_shape=jax.ShapeDtypeStruct((PS, CH, 16,...]
    pallas_call x1, Pallas kernels: 19.6 us -> 5.35 us  [per_device(): pl.pallas_call(gradient_kernel, out_shape=jax.ShapeDtypeStruct((AUG, MROW...]
    transpose x0 -> x1, local copies, waits for them, and re-layouts: none -> 2.23 us  [per_device(): blocks = out_grads[0, 0].T.reshape(AUG, COLS, GRID * GRID)]
    pallas_call x1, Pallas kernels: 1.87 us -> 0.33 us  [per_device(): pl.pallas_call(shard_kernel, out_shape=(jax.ShapeDtypeStruct((ROWS, LANES...]
    reshape x1 -> x0, local copies, waits for them, and re-layouts: 1.3 us -> none  [per_device(): blocks = wide.reshape(GRID * GRID, AUG, LANES).transpose(1, 0, 2)]
    unnamed x13 -> x10, local copies, waits for them, and re-layouts: 3.6 us -> 4.08 us
  transfers between devices with their start and end apart: 3 -> 3, of which waited for: 3 -> 3; matrix products, arithmetic and copies ran while one was open for 1% -> 1% of each run, Pallas kernels for 0% -> 15%
where the time goes in v2:
time: 100 us; the launch traced here: 99.8 us
  waiting for transfers between devices  27.5 us (28%)
  blocking collectives  23.9 us (24%)
  Pallas kernels  20.9 us (21%)
  starting transfers between devices  17.6 us (18%)
  local copies, waits for them, and re-layouts  8.3 us (8%)
    all_to_all x1, blocking collectives, per_device(): pieces = lax.all_to_all(term.reshape(images_in_all, -1, LANES), 'dp', 0, 0)  23.9 us
    pallas_call x1, Pallas kernels, per_device(): pl.pallas_call(patch_kernel, out_shape=jax.ShapeDtypeStruct((PS, CH, 16,...  15.2 us
    all_to_all x1, waiting for transfers between devices, per_device(): parts = lax.all_to_all(parts, 'aug', 0, 0)  12.9 us
    all_to_all x1, waiting for transfers between devices, per_device(): clipped_sum = lax.all_to_all(spread, 'dp', 0, 0).reshape(-1)[:SHARD]  10.7 us
    all_to_all x1, starting transfers between devices, per_device(): blocks = lax.all_to_all(blocks, 'aug', 0, 0)  10.3 us
    pallas_call x1, Pallas kernels, per_device(): pl.pallas_call(gradient_kernel, out_shape=jax.ShapeDtypeStruct((AUG, MROW...  5.35 us
    unnamed x10, local copies, waits for them, and re-layouts  4.08 us
    all_to_all x1, waiting for transfers between devices, per_device(): blocks = lax.all_to_all(blocks, 'aug', 0, 0)  3.96 us
  transfers between devices with their start and end apart: 3, of which 3 were waited for; matrix products, arithmetic and copies ran while one was open for 1% of the time, Pallas kernels for 15%

profile of v2, /device:TPU:1, one launch (start us, length us, event | category | flops | bytes accessed | tf_op | source)
XLA Modules:
  0.0 99.8 jit_solution(1255016134076634032)
XLA Ops:
  0.6 2.2 %copy.10 = bf16[1664,256]{1,0:T(8,128)(2,1)} copy(bf16[1664,256]{0,1:T(8,128)(2,1)} %bitcast.15) | data formatting | bytes 1703936 | tf_op jit(solution)/shard_map/transpose | solution.py:150
  2.9 10.3 %all-to-all-start = ((bf16[16,104,256]{2,1,0:T(8,128)(2,1)}), bf16[16,104,256]{2,1,0:T(8,128)(2,1)S(1)}, u32[]{:S(2)}, u32[]{:S(2)}) async-start(bf16[16,104,256]{2,1,0:T(8,128)(2,1)} %bitcast.6), calls=%async_computation | async-start | bytes 1703936 | tf_op jit(solution)/shard_map/all_to_all | solution.py:151
  13.1 0.8 copy.9.offs
  13.9 0.0 copy-start.1
  13.9 1.0 copy-done.1
  14.9 0.0 copy-start.2
  14.9 0.7 copy-done.2
  15.6 15.2 %shard_map.85.pat = bf16[14,3,16,4096]{3,2,1,0:T(8,128)(2,1)S(1)} custom-call(s32[16,2]{1,0:T(8,128)S(1)} %copy.9.offs, s32[16]{0:T(128)S(1)} %bitcast.13, bf16[3,256,256]{2,1,0:T(8,128)(2,1)S(1)} %bitcast.12), custom_call_target="tpu_custom_call" | custom-call | flops 20000000000 | bytes 20000000 | tf_op jit(solution)/shard_map/pallas_call | solution.py:152
  30.8 0.0 copy-start
  30.8 2.4 %copy-done = bf16[14,3,16,4096]{3,2,1,0:T(8,128)(2,1)} copy-done((bf16[14,3,16,4096]{3,2,1,0:T(8,128)(2,1)}, bf16[14,3,16,4096]{3,2,1,0:T(8,128)(2,1)S(1)}, u32[]{:S(2)}) %copy-start) | copy-done | bytes 5505048
  33.2 0.0 copy-start.3
  33.2 0.0 copy-start.4
  33.2 4.0 %all-to-all-done.grads = bf16[16,104,256]{2,1,0:T(8,128)(2,1)S(1)} async-done(((bf16[16,104,256]{2,1,0:T(8,128)(2,1)}), bf16[16,104,256]{2,1,0:T(8,128)(2,1)S(1)}, u32[]{:S(2)}, u32[]{:S(2)}) %all-to-all-start) | async-done | bytes 852000 | tf_op jit(solution)/shard_map/all_to_all | solution.py:151
  37.2 5.4 %shard_map.86 = f32[16,40,128]{2,1,0:T(8,128)} custom-call(bf16[14,3,16,4096]{3,2,1,0:T(8,128)(2,1)} %copy-done, bf16[16,104,256]{2,1,0:T(8,128)(2,1)S(1)} %all-to-all-done.grads), custom_call_target="tpu_custom_call" | custom-call | tf_op jit(solution)/shard_map/pallas_call | solution.py:167
  42.5 3.5 %all-to-all-start.1 = ((f32[16,40,128]{2,1,0:T(8,128)}), f32[16,40,128]{2,1,0:T(8,128)S(1)}, u32[]{:S(2)}, u32[]{:S(2)}) async-start(f32[16,40,128]{2,1,0:T(8,128)} %shard_map.86), calls=%async_computation.1 | async-start | bytes 655360 | tf_op jit(solution)/shard_map/all_to_all | solution.py:180
  46.0 12.9 %all-to-all-done.1.parts = f32[16,40,128]{2,1,0:T(8,128)S(1)} async-done(((f32[16,40,128]{2,1,0:T(8,128)}), f32[16,40,128]{2,1,0:T(8,128)S(1)}, u32[]{:S(2)}, u32[]{:S(2)}) %all-to-all-start.1) | async-done | bytes 327712 | tf_op jit(solution)/shard_map/all_to_all | solution.py:180
  58.9 0.3 shard_map.87
  59.3 23.9 %all_to_all.20 = f32[32,16,128]{2,1,0:T(8,128)S(1)} all-to-all(f32[32,16,128]{2,1,0:T(8,128)S(1)} %bitcast.11), channel_id=1, replica_groups=mesh['dp'=32,'aug'=16] {'dp'}, dimensions={0} | all-to-all | bytes 524288 | tf_op jit(solution)/shard_map/all_to_all | solution.py:192
  83.2 0.7 broadcast_in_dim.2
  84.0 3.9 %all-to-all-start.3 = ((f32[32,16,128]{2,1,0:T(8,128)}), f32[32,16,128]{2,1,0:T(8,128)S(1)}, u32[]{:S(2)}, u32[]{:S(2)}) async-start(f32[32,16,128]{2,1,0:T(8,128)} %broadcast_in_dim.2), calls=%async_computation.3 | async-start | bytes 524288 | tf_op jit(solution)/shard_map/all_to_all | solution.py:195
  87.8 0.5 slice.7
  88.3 10.7 %all-to-all-done.3 = f32[32,16,128]{2,1,0:T(8,128)S(1)} async-done(((f32[32,16,128]{2,1,0:T(8,128)}), f32[32,16,128]{2,1,0:T(8,128)S(1)}, u32[]{:S(2)}, u32[]{:S(2)}) %all-to-all-start.3) | async-done | bytes 262176 | tf_op jit(solution)/shard_map/all_to_all | solution.py:195
  99.0 0.0 copy-done.3
  99.0 0.0 copy-done.4
  99.0 0.8 slice_multiply_fusion
  (1 shorter events, 0.0 us)
Async XLA Ops:
  2.9 34.3 %all-to-all-start = ((bf16[16,104,256]{2,1,0:T(8,128)(2,1)}), bf16[16,104,256]{2,1,0:T(8,128)(2,1)S(1)}, u32[]{:S(2)}, u32[]{:S(2)}) async-start(bf16[16,104,256]{2,1,0:T(8,128)(2,1)} %bitcast.6), calls=%async_computation | async-start | bytes 1703936 | tf_op jit(solution)/shard_map/all_to_all | solution.py:151
  13.9 1.0 copy-start.1
  14.9 0.7 copy-start.2
  30.8 2.4 %copy-start = (bf16[14,3,16,4096]{3,2,1,0:T(8,128)(2,1)}, bf16[14,3,16,4096]{3,2,1,0:T(8,128)(2,1)S(1)}, u32[]{:S(2)}) copy-start(bf16[14,3,16,4096]{3,2,1,0:T(8,128)(2,1)S(1)} %shard_map.85.pat) | copy-start | bytes 16515076
  33.2 65.8 %copy-start.3 = (f32[61152]{0:T(1024)S(1)}, f32[61152]{0:T(1024)}, u32[]{:S(2)}) copy-start(f32[61152]{0:T(1024)} %param.10) | copy-start | bytes 733828
  33.2 65.8 %copy-start.4 = (f32[61152]{0:T(1024)S(1)}, f32[61152]{0:T(1024)}, u32[]{:S(2)}) copy-start(f32[61152]{0:T(1024)} %param.11) | copy-start | bytes 733828
  42.5 16.4 %all-to-all-start.1 = ((f32[16,40,128]{2,1,0:T(8,128)}), f32[16,40,128]{2,1,0:T(8,128)S(1)}, u32[]{:S(2)}, u32[]{:S(2)}) async-start(f32[16,40,128]{2,1,0:T(8,128)} %shard_map.86), calls=%async_computation.1 | async-start | bytes 655360 | tf_op jit(solution)/shard_map/all_to_all | solution.py:180
  84.0 15.0 %all-to-all-start.3 = ((f32[32,16,128]{2,1,0:T(8,128)}), f32[32,16,128]{2,1,0:T(8,128)S(1)}, u32[]{:S(2)}, u32[]{:S(2)}) async-start(f32[32,16,128]{2,1,0:T(8,128)} %broadcast_in_dim.2), calls=%async_computation.3 | async-start | bytes 524288 | tf_op jit(solution)/shard_map/all_to_all | solution.py:195

commit v3 on v2

--- a/solution.py
+++ b/solution.py
@@ -21,8 +21,13 @@
 CLIP = math.sqrt(PATCH * D)
 SHARD = PATCH * D // AUG
 SROWS = 38
-MROWS = 40
-ROWS = 512
+MROWS = 48
+PROWS = 15
+ROWS = 480
+FULL = 32700.0
+LEVELS = 256.0
+COARSE = 64.0
+FINE = 1e6
 SPARE = 8
 MIB = 1024 * 1024
 PITCH = SIDE + SPARE
@@ -93,6 +98,7 @@
 def gradient_kernel(pat, grads, msg, near, gord, flat, sem):
     fetch = pltpu.make_async_copy(pat, near, sem)
     fetch.start()
+    flat[...] = jnp.zeros(flat.shape, jnp.float32)
     for k in range(AUG):
         turned = grads[k].T
         for y in range(GRID):
@@ -105,19 +111,47 @@
             first = v * CH * 16 + c * 16
             flat[pl.ds(c * PS * PS + v, PS, stride=PS), 0:COLS] = total[first:first + PS, :]
 
-    flat[PATCH:, 0:COLS] = jnp.zeros((4, COLS), jnp.float32)
     values = flat[:, 0:COLS]
-    squares = jnp.sum(values * values)
+    squares = jnp.full((1, LANES), jnp.sum(values * values), jnp.float32)
+    coarse = jnp.floor(jnp.log(jnp.maximum(squares, 1e-36)) * COARSE)
+    fine = (squares / jnp.exp(coarse / COARSE) - 1.0) * FINE
+    row = lax.broadcasted_iota(jnp.int32, (MROWS, LANES), 0)
+    inside = (row < SROWS) & (lax.broadcasted_iota(jnp.int32, (MROWS, LANES), 1) < COLS)
+    tail = jnp.where(row == SROWS + 1, coarse, jnp.where(row == SROWS + 2, rounded(fine), 0.0))
     for b in range(AUG):
         first = 147 * b // 4
-        msg[b, 0:SROWS, 0:COLS] = flat[first:first + SROWS, 0:COLS]
-        msg[b, SROWS:MROWS, :] = jnp.full((MROWS - SROWS, LANES), squares, jnp.float32)
-
-
-def shard_kernel(index, parts, term, norm, lined):
+        block = jnp.where(inside, flat[first:first + MROWS, :], 0.0)
+        codes, level = encode(block, jnp.abs(block))
+        codes = jnp.where(row < SROWS, codes, jnp.where(row == SROWS, level, tail))
+        msg[b] = codes.astype(jnp.int32).astype(jnp.int16)
+
+
+def rounded(value):
+    return jnp.clip(jnp.floor(value + 0.5), -32767.0, 32767.0)
+
+
+def encode(block, sizes):
+    most = jnp.max(sizes, axis=0, keepdims=True)
+    level = jnp.ceil(jnp.log(jnp.maximum(most, 1e-30)) * LEVELS)
+    return rounded(block * (FULL * jnp.exp(level * (-1.0 / LEVELS)))), level
+
+
+def step_of(level):
+    return jnp.exp(level * (1.0 / LEVELS)) * (1.0 / FULL)
+
+
+def plain(codes):
+    return codes.astype(jnp.int32).astype(jnp.float32)
+
+
+def shard_kernel(index, parts, term, norm, lined, even):
     squares = jnp.zeros((1, LANES), jnp.float32)
+    opened = []
     for a in range(AUG):
-        squares = squares + parts[a, SROWS:SROWS + 1, :]
+        part = plain(parts[a])
+        opened.append(part[0:SROWS] * step_of(part[SROWS:SROWS + 1]))
+        coarse, fine = part[SROWS + 1:SROWS + 2], part[SROWS + 2:SROWS + 3]
+        squares = squares + jnp.exp(coarse / COARSE) * (1.0 + fine / FINE)
     length = jnp.sqrt(squares / (AUG * AUG) + 1e-6)
     norm[...] = jnp.broadcast_to(length, (8, LANES))
     scale = jnp.minimum(1.0, CLIP / length) / AUG
@@ -126,7 +160,7 @@
         value = None
         for a in range(LANES * block // COLS, (LANES * block + LANES - 1) // COLS + 1):
             begin = a * COLS - LANES * block
-            piece = pltpu.roll(parts[a, 0:SROWS, :], begin % LANES, 1) * scale
+            piece = pltpu.roll(opened[a], begin % LANES, 1) * scale
             value = piece if value is None else jnp.where(lane >= begin, piece, value)
         lined[pl.ds(block, SROWS, stride=BLOCKS), :] = value
     lined[SROWS * BLOCKS:, :] = jnp.zeros((lined.shape[0] - SROWS * BLOCKS, LANES), jnp.float32)
@@ -137,7 +171,36 @@
     far = lined[pl.ds(rows + 1, ROWS), :]
     lane = lax.broadcasted_iota(jnp.int32, (ROWS, LANES), 1)
     mixed = jnp.where(lane >= lanes, near, far)
-    term[...] = pltpu.roll(mixed, (LANES - lanes) % LANES, 1)
+    even[0:ROWS, :] = pltpu.roll(mixed, (LANES - lanes) % LANES, 1)
+    even[ROWS:, :] = jnp.zeros((8, LANES), jnp.float32)
+    place = lax.broadcasted_iota(jnp.int32, (8, LANES), 0) * LANES + lax.broadcasted_iota(jnp.int32, (8, LANES), 1)
+    inside = place < SHARD - (ROWS - 8) * LANES
+    even[ROWS - 8:ROWS, :] = jnp.where(inside, even[ROWS - 8:ROWS, :], 0.0)
+    for j in range(term.shape[0]):
+        term[j] = coded_chunk(even[PROWS * j:PROWS * j + 16, :])
+
+
+def coded_chunk(block):
+    row = lax.broadcasted_iota(jnp.int32, (16, LANES), 0)
+    codes, level = encode(block, jnp.where(row < PROWS, jnp.abs(block), 0.0))
+    return jnp.where(row < PROWS, codes, level).astype(jnp.int32).astype(jnp.int16)
+
+
+def total_kernel(pieces, spread):
+    total = jnp.zeros((16, LANES), jnp.float32)
+    for i in range(pieces.shape[0]):
+        piece = plain(pieces[i])
+        total = total + piece * step_of(piece[PROWS:PROWS + 1])
+    codes = coded_chunk(total)
+    for j in range(spread.shape[0]):
+        spread[j] = codes
+
+
+def open_kernel(chunks, shard):
+    for j in range(chunks.shape[0]):
+        chunk = plain(chunks[j])
+        value = chunk * step_of(chunk[PROWS:PROWS + 1])
+        shard[PROWS * j:PROWS * (j + 1), :] = value[0:PROWS]
 
 
 VMEM = pl.BlockSpec(memory_space=pltpu.VMEM)
@@ -166,33 +229,47 @@
     )(offsets[0], flip_flags[0], images[0])
     parts = pl.pallas_call(
         gradient_kernel,
-        out_shape=jax.ShapeDtypeStruct((AUG, MROWS, LANES), jnp.float32),
+        out_shape=jax.ShapeDtypeStruct((AUG, MROWS, LANES), jnp.int16),
         in_specs=[pl.BlockSpec(memory_space=pl.ANY), VMEM],
         out_specs=VMEM,
         scratch_shapes=[
             pltpu.VMEM((PS, CH, 16, AUG * SIDE), jnp.bfloat16),
             pltpu.VMEM((AUG * SIDE, COLS), jnp.bfloat16),
-            pltpu.VMEM((PATCH + 4, LANES), jnp.float32),
+            pltpu.VMEM((PATCH + 12, LANES), jnp.float32),
             pltpu.SemaphoreType.DMA,
         ],
         compiler_params=pltpu.CompilerParams(vmem_limit_bytes=48 * MIB),
     )(pat, blocks)
     parts = lax.all_to_all(parts, "aug", 0, 0)
+    chunks = jax.ShapeDtypeStruct((images_in_all, 16, LANES), jnp.int16)
     term, norm = pl.pallas_call(
         shard_kernel,
-        out_shape=(
-            jax.ShapeDtypeStruct((ROWS, LANES), jnp.float32),
-            jax.ShapeDtypeStruct((8, LANES), jnp.float32),
-        ),
+        out_shape=(chunks, jax.ShapeDtypeStruct((8, LANES), jnp.float32)),
         in_specs=[SMEM, VMEM],
         out_specs=(VMEM, VMEM),
-        scratch_shapes=[pltpu.VMEM((ROWS + 16, LANES), jnp.float32)],
+        scratch_shapes=[
+            pltpu.VMEM((ROWS + 32, LANES), jnp.float32),
+            pltpu.VMEM((ROWS + 8, LANES), jnp.float32),
+        ],
         compiler_params=pltpu.CompilerParams(vmem_limit_bytes=8 * MIB),
     )(aug_index.reshape(1), parts)
-    pieces = lax.all_to_all(term.reshape(images_in_all, -1, LANES), "dp", 0, 0)
-    piece = jnp.sum(pieces, axis=0)
-    spread = jnp.broadcast_to(piece[None], pieces.shape)
-    clipped_sum = lax.all_to_all(spread, "dp", 0, 0).reshape(-1)[:SHARD]
+    pieces = lax.all_to_all(term, "dp", 0, 0)
+    spread = pl.pallas_call(
+        total_kernel,
+        out_shape=chunks,
+        in_specs=[VMEM],
+        out_specs=VMEM,
+        compiler_params=pltpu.CompilerParams(vmem_limit_bytes=8 * MIB),
+    )(pieces)
+    gathered = lax.all_to_all(spread, "dp", 0, 0)
+    shard = pl.pallas_call(
+        open_kernel,
+        out_shape=jax.ShapeDtypeStruct((ROWS, LANES), jnp.float32),
+        in_specs=[VMEM],
+        out_specs=VMEM,
+        compiler_params=pltpu.CompilerParams(vmem_limit_bytes=8 * MIB),
+    )(gathered)
+    clipped_sum = shard.reshape(-1)[:SHARD]
     clipped_mean = clipped_sum / images_in_all
     new_weight = weight - 0.1 * (clipped_sum / CLIP + gauss_noise)
     return (new_weight, clipped_mean, norm[0, 0:1])

time: 100 us -> 93 us (0.930)
  waiting for transfers between devices: 27.5 us -> 23 us
  blocking collectives: 23.9 us -> 20.9 us
    all_to_all x1, blocking collectives: 23.9 us -> 20.9 us  [per_device(): pieces = lax.all_to_all(term, 'dp', 0, 0)]
    all_to_all x1, waiting for transfers between devices: 12.9 us -> 10.2 us  [per_device(): parts = lax.all_to_all(parts, 'aug', 0, 0)]
    all_to_all x1, waiting for transfers between devices: 10.7 us -> 8.9 us  [per_device(): gathered = lax.all_to_all(spread, 'dp', 0, 0)]
  transfers between devices with their start and end apart: 3 -> 3, of which waited for: 3 -> 3; matrix products, arithmetic and copies ran while one was open for 1% -> 1% of each run, Pallas kernels for 15% -> 16%
where the time goes in v3:
time: 93 us; the launch traced here: 92.5 us
  waiting for transfers between devices  23 us (25%)
  Pallas kernels  21.8 us (23%)
  blocking collectives  20.9 us (22%)
  starting transfers between devices  17.6 us (19%)
  local copies, waits for them, and re-layouts  7.56 us (8%)
    all_to_all x1, blocking collectives, per_device(): pieces = lax.all_to_all(term, 'dp', 0, 0)  20.9 us
    pallas_call x1, Pallas kernels, per_device(): pl.pallas_call(patch_kernel, out_shape=jax.ShapeDtypeStruct((PS, CH, 16,...  15.2 us
    all_to_all x1, starting transfers between devices, per_device(): blocks = lax.all_to_all(blocks, 'aug', 0, 0)  10.3 us
    all_to_all x1, waiting for transfers between devices, per_device(): parts = lax.all_to_all(parts, 'aug', 0, 0)  10.2 us
    all_to_all x1, waiting for transfers between devices, per_device(): gathered = lax.all_to_all(spread, 'dp', 0, 0)  8.9 us
    pallas_call x1, Pallas kernels, per_device(): pl.pallas_call(gradient_kernel, out_shape=jax.ShapeDtypeStruct((AUG, MROW...  5.37 us
    unnamed x10, local copies, waits for them, and re-layouts  4.07 us
    all_to_all x1, waiting for transfers between devices, per_device(): blocks = lax.all_to_all(blocks, 'aug', 0, 0)  3.97 us
  transfers between devices with their start and end apart: 3, of which 3 were waited for; matrix products, arithmetic and copies ran while one was open for 1% of the time, Pallas kernels for 16%

profile of v3, /device:TPU:1, one launch (start us, length us, event | category | flops | bytes accessed | tf_op | source)
XLA Modules:
  0.0 92.5 jit_solution(5249065484566730472)
XLA Ops:
  0.6 2.2 %copy.10 = bf16[1664,256]{1,0:T(8,128)(2,1)} copy(bf16[1664,256]{0,1:T(8,128)(2,1)} %bitcast.13) | data formatting | bytes 1703936 | tf_op jit(solution)/shard_map/transpose | solution.py:213
  2.9 10.3 %all-to-all-start = ((bf16[16,104,256]{2,1,0:T(8,128)(2,1)}), bf16[16,104,256]{2,1,0:T(8,128)(2,1)S(1)}, u32[]{:S(2)}, u32[]{:S(2)}) async-start(bf16[16,104,256]{2,1,0:T(8,128)(2,1)} %bitcast.6), calls=%async_computation | async-start | bytes 1703936 | tf_op jit(solution)/shard_map/all_to_all | solution.py:214
  13.1 0.8 copy.9.offs
  13.9 0.0 copy-start.1
  13.9 1.0 %copy-done.1 = bf16[1,3,256,256]{3,2,1,0:T(8,128)(2,1)S(1)} copy-done((bf16[1,3,256,256]{3,2,1,0:T(8,128)(2,1)S(1)}, bf16[1,3,256,256]{3,2,1,0:T(8,128)(2,1)}, u32[]{:S(2)}) %copy-start.1) | copy-done | bytes 393240
  14.9 0.0 copy-start.2
  14.9 0.7 copy-done.2
  15.6 15.2 %shard_map.85.pat = bf16[14,3,16,4096]{3,2,1,0:T(8,128)(2,1)S(1)} custom-call(s32[16,2]{1,0:T(8,128)S(1)} %copy.9.offs, s32[16]{0:T(128)S(1)} %bitcast.12, bf16[3,256,256]{2,1,0:T(8,128)(2,1)S(1)} %bitcast.11), custom_call_target="tpu_custom_call" | custom-call | flops 20000000000 | bytes 20000000 | tf_op jit(solution)/shard_map/pallas_call | solution.py:215
  30.8 0.0 copy-start
  30.8 2.4 %copy-done = bf16[14,3,16,4096]{3,2,1,0:T(8,128)(2,1)} copy-done((bf16[14,3,16,4096]{3,2,1,0:T(8,128)(2,1)}, bf16[14,3,16,4096]{3,2,1,0:T(8,128)(2,1)S(1)}, u32[]{:S(2)}) %copy-start) | copy-done | bytes 5505048
  33.2 0.0 copy-start.3
  33.2 0.0 copy-start.4
  33.2 4.0 %all-to-all-done.grads = bf16[16,104,256]{2,1,0:T(8,128)(2,1)S(1)} async-done(((bf16[16,104,256]{2,1,0:T(8,128)(2,1)}), bf16[16,104,256]{2,1,0:T(8,128)(2,1)S(1)}, u32[]{:S(2)}, u32[]{:S(2)}) %all-to-all-start) | async-done | bytes 852000 | tf_op jit(solution)/shard_map/all_to_all | solution.py:214
  37.2 5.4 %shard_map.86 = s16[16,48,128]{2,1,0:T(8,128)(2,1)} custom-call(bf16[14,3,16,4096]{3,2,1,0:T(8,128)(2,1)} %copy-done, bf16[16,104,256]{2,1,0:T(8,128)(2,1)S(1)} %all-to-all-done.grads), custom_call_target="tpu_custom_call" | custom-call | tf_op jit(solution)/shard_map/pallas_call | solution.py:230
  42.5 3.4 %all-to-all-start.1 = ((s16[16,48,128]{2,1,0:T(8,128)(2,1)}), s16[16,48,128]{2,1,0:T(8,128)(2,1)S(1)}, u32[]{:S(2)}, u32[]{:S(2)}) async-start(s16[16,48,128]{2,1,0:T(8,128)(2,1)} %shard_map.86), calls=%async_computation.1 | async-start | bytes 393216 | tf_op jit(solution)/shard_map/all_to_all | solution.py:243
  46.0 10.2 %all-to-all-done.1.parts = s16[16,48,128]{2,1,0:T(8,128)(2,1)S(1)} async-done(((s16[16,48,128]{2,1,0:T(8,128)(2,1)}), s16[16,48,128]{2,1,0:T(8,128)(2,1)S(1)}, u32[]{:S(2)}, u32[]{:S(2)}) %all-to-all-start.1) | async-done | bytes 196640 | tf_op jit(solution)/shard_map/all_to_all | solution.py:243
  56.2 0.4 shard_map.87
  56.6 20.9 %all_to_all.20.pieces = s16[32,16,128]{2,1,0:T(8,128)(2,1)S(1)} all-to-all(s16[32,16,128]{2,1,0:T(8,128)(2,1)S(1)} %get-tuple-element.5), channel_id=1, replica_groups=mesh['dp'=32,'aug'=16] {'dp'}, dimensions={0} | all-to-all | bytes 262144 | tf_op jit(solution)/shard_map/all_to_all | solution.py:256
  77.5 0.8 shard_map.88
  78.3 3.9 %all-to-all-start.3 = ((s16[32,16,128]{2,1,0:T(8,128)(2,1)}), s16[32,16,128]{2,1,0:T(8,128)(2,1)S(1)}, u32[]{:S(2)}, u32[]{:S(2)}) async-start(s16[32,16,128]{2,1,0:T(8,128)(2,1)} %shard_map.88), calls=%async_computation.3 | async-start | bytes 262144 | tf_op jit(solution)/shard_map/all_to_all | solution.py:264
  82.1 0.5 slice.7
  82.7 8.9 %all-to-all-done.3.chunks = s16[32,16,128]{2,1,0:T(8,128)(2,1)S(1)} async-done(((s16[32,16,128]{2,1,0:T(8,128)(2,1)}), s16[32,16,128]{2,1,0:T(8,128)(2,1)S(1)}, u32[]{:S(2)}, u32[]{:S(2)}) %all-to-all-start.3) | async-done | bytes 131104 | tf_op jit(solution)/shard_map/all_to_all | solution.py:264
  91.6 0.1 shard_map.89
  91.6 0.0 copy-done.3
  91.6 0.0 copy-done.4
  91.6 0.8 slice_multiply_fusion
Async XLA Ops:
  2.9 34.3 %all-to-all-start = ((bf16[16,104,256]{2,1,0:T(8,128)(2,1)}), bf16[16,104,256]{2,1,0:T(8,128)(2,1)S(1)}, u32[]{:S(2)}, u32[]{:S(2)}) async-start(bf16[16,104,256]{2,1,0:T(8,128)(2,1)} %bitcast.6), calls=%async_computation | async-start | bytes 1703936 | tf_op jit(solution)/shard_map/all_to_all | solution.py:214
  13.9 1.0 %copy-start.1 = (bf16[1,3,256,256]{3,2,1,0:T(8,128)(2,1)S(1)}, bf16[1,3,256,256]{3,2,1,0:T(8,128)(2,1)}, u32[]{:S(2)}) copy-start(bf16[1,3,256,256]{3,2,1,0:T(8,128)(2,1)} %param.6) | copy-start | bytes 1179652
  14.9 0.7 copy-start.2
  30.8 2.4 %copy-start = (bf16[14,3,16,4096]{3,2,1,0:T(8,128)(2,1)}, bf16[14,3,16,4096]{3,2,1,0:T(8,128)(2,1)S(1)}, u32[]{:S(2)}) copy-start(bf16[14,3,16,4096]{3,2,1,0:T(8,128)(2,1)S(1)} %shard_map.85.pat) | copy-start | bytes 16515076
  33.2 58.4 %copy-start.3 = (f32[61152]{0:T(1024)S(1)}, f32[61152]{0:T(1024)}, u32[]{:S(2)}) copy-start(f32[61152]{0:T(1024)} %param.10) | copy-start | bytes 733828
  33.2 58.4 %copy-start.4 = (f32[61152]{0:T(1024)S(1)}, f32[61152]{0:T(1024)}, u32[]{:S(2)}) copy-start(f32[61152]{0:T(1024)} %param.11) | copy-start | bytes 733828
  42.5 13.6 %all-to-all-start.1 = ((s16[16,48,128]{2,1,0:T(8,128)(2,1)}), s16[16,48,128]{2,1,0:T(8,128)(2,1)S(1)}, u32[]{:S(2)}, u32[]{:S(2)}) async-start(s16[16,48,128]{2,1,0:T(8,128)(2,1)} %shard_map.86), calls=%async_computation.1 | async-start | bytes 393216 | tf_op jit(solution)/shard_map/all_to_all | solution.py:243
  78.3 13.3 %all-to-all-start.3 = ((s16[32,16,128]{2,1,0:T(8,128)(2,1)}), s16[32,16,128]{2,1,0:T(8,128)(2,1)S(1)}, u32[]{:S(2)}, u32[]{:S(2)}) async-start(s16[32,16,128]{2,1,0:T(8,128)(2,1)} %shard_map.88), calls=%async_computation.3 | async-start | bytes 262144 | tf_op jit(solution)/shard_map/all_to_all | solution.py:264

commit v4 on v3

--- a/solution.py
+++ b/solution.py
@@ -30,10 +30,12 @@
 FINE = 1e6
 SPARE = 8
 MIB = 1024 * 1024
+EARLY = 7
+ORDER = list(range(0, AUG, 2)) + list(range(1, AUG, 2))
 PITCH = SIDE + SPARE
 
 
-def patch_kernel(offs, flags, img, pat, sel, cols, held):
+def patch_kernel(offs, flags, img, pat_early, pat_late, sel, cols):
     lane = lax.broadcasted_iota(jnp.int32, (SIDE, SIDE), 1)
     row = lax.broadcasted_iota(jnp.int32, (SIDE, SIDE), 0)
     slot = lane // 16
@@ -56,56 +58,62 @@
                 cols[c, 2 * k + h, 0:SIDE, :] = picked[:, h * LANES:(h + 1) * LANES]
             cols[c, 2 * k:2 * k + 2, SIDE:, :] = jnp.zeros((2, SPARE, LANES), jnp.float32)
 
-    slots = lax.broadcasted_iota(jnp.int32, (8, LANES), 1) // 16
+    slots = lax.broadcasted_iota(jnp.int32, (16, LANES), 1) // 16
     masks = [slots == s for s in range(8)]
 
-    def assemble(step, carry):
-        c = step // GRID
-        y = step % GRID
-        for half in range(2):
-            parts = []
-            for k in range(AUG):
-                start = offs[k, 0] + PS * y + 8 * half
-                parts.append([cols[c, 2 * k + h, pl.ds(start, 8), :] for h in range(2)])
-            for v in range(PS):
-                pair = []
-                for h in range(2):
-                    value = None
-                    for s in range(8):
-                        k = (8 * h + s - v) % 16
-                        piece = parts[k][h]
-                        value = piece if value is None else jnp.where(masks[s], piece, value)
-                    pair.append(value)
-                shift = 16 * v
-                turn = shift % LANES
-                if turn:
-                    low = pltpu.roll(pair[0], LANES - turn, 1)
-                    high = pltpu.roll(pair[1], LANES - turn, 1)
-                    keep = slots < (LANES - turn) // 16
-                    pair = [jnp.where(keep, low, high), jnp.where(keep, high, low)]
-                if shift >= LANES:
-                    pair = pair[::-1]
-                for h in range(2):
-                    held[v, 8 * half:8 * half + 8, h * LANES:(h + 1) * LANES] = pair[h]
+    def assemble(pat, begin, count, step, carry):
+        c = step // count
+        place_y = step % count
+        y = begin + place_y
+        parts = []
+        for k in range(AUG):
+            rows = pl.ds(offs[k, 0] + PS * y, 16)
+            parts.append([cols[c, 2 * k + h, rows, :].astype(jnp.bfloat16) for h in range(2)])
         for v in range(PS):
-            place = pl.ds(pl.multiple_of(y * SIDE, SIDE), SIDE)
-            pat[v, c, :, place] = held[v].astype(jnp.bfloat16)
+            pair = []
+            for h in range(2):
+                value = None
+                for s in range(8):
+                    piece = parts[(8 * h + s - v) % 16][h]
+                    value = piece if value is None else jnp.where(masks[s], piece, value)
+                pair.append(value)
+            shift = 16 * v
+            turn = shift % LANES
+            if turn:
+                low = pltpu.roll(pair[0], LANES - turn, 1)
+                high = pltpu.roll(pair[1], LANES - turn, 1)
+                keep = slots < (LANES - turn) // 16
+                pair = [jnp.where(keep, low, high), jnp.where(keep, high, low)]
+            if shift >= LANES:
+                pair = pair[::-1]
+            for h in range(2):
+                place = pl.ds(pl.multiple_of(place_y * SIDE + h * LANES, LANES), LANES)
+                pat[v, c, :, place] = pair[h]
         return carry
 
-    lax.fori_loop(0, CH * GRID, assemble, 0)
-
-
-def gradient_kernel(pat, grads, msg, near, gord, flat, sem):
-    fetch = pltpu.make_async_copy(pat, near, sem)
+    for pat, begin, count in ((pat_early, 0, EARLY), (pat_late, EARLY, GRID - EARLY)):
+        lax.fori_loop(0, CH * count, functools.partial(assemble, pat, begin, count), 0)
+
+
+def gradient_kernel(pat_early, pat_late, grads, msg, near, gord, flat, sem):
+    fetch = pltpu.make_async_copy(pat_late, near, sem)
     fetch.start()
     flat[...] = jnp.zeros(flat.shape, jnp.float32)
     for k in range(AUG):
         turned = grads[k].T
         for y in range(GRID):
             gord[(y * AUG + k) * 16:(y * AUG + k + 1) * 16, :] = turned[y * 16:(y + 1) * 16, :]
+    total = jnp.dot(
+        pat_early[...].reshape(PS * CH * 16, EARLY * SIDE),
+        gord[0:EARLY * SIDE, :],
+        preferred_element_type=jnp.float32,
+    )
     fetch.wait()
-    left = near[...].reshape(PS * CH * 16, AUG * SIDE)
-    total = jnp.dot(left, gord[...], preferred_element_type=jnp.float32)
+    total = total + jnp.dot(
+        near[...].reshape(PS * CH * 16, (GRID - EARLY) * SIDE),
+        gord[EARLY * SIDE:, :],
+        preferred_element_type=jnp.float32,
+    )
     for v in range(PS):
         for c in range(CH):
             first = v * CH * 16 + c * 16
@@ -118,12 +126,12 @@
     row = lax.broadcasted_iota(jnp.int32, (MROWS, LANES), 0)
     inside = (row < SROWS) & (lax.broadcasted_iota(jnp.int32, (MROWS, LANES), 1) < COLS)
     tail = jnp.where(row == SROWS + 1, coarse, jnp.where(row == SROWS + 2, rounded(fine), 0.0))
-    for b in range(AUG):
+    for order, b in enumerate(ORDER):
         first = 147 * b // 4
         block = jnp.where(inside, flat[first:first + MROWS, :], 0.0)
         codes, level = encode(block, jnp.abs(block))
         codes = jnp.where(row < SROWS, codes, jnp.where(row == SROWS, level, tail))
-        msg[b] = codes.astype(jnp.int32).astype(jnp.int16)
+        msg[order] = codes.astype(jnp.int32).astype(jnp.int16)
 
 
 def rounded(value):
@@ -148,7 +156,7 @@
     squares = jnp.zeros((1, LANES), jnp.float32)
     opened = []
     for a in range(AUG):
-        part = plain(parts[a])
+        part = plain(parts[ORDER.index(a)])
         opened.append(part[0:SROWS] * step_of(part[SROWS:SROWS + 1]))
         coarse, fine = part[SROWS + 1:SROWS + 2], part[SROWS + 2:SROWS + 3]
         squares = squares + jnp.exp(coarse / COARSE) * (1.0 + fine / FINE)
@@ -212,17 +220,19 @@
     images_in_all = lax.axis_size("dp")
     blocks = out_grads[0, 0].T.reshape(AUG, COLS, GRID * GRID)
     blocks = lax.all_to_all(blocks, "aug", 0, 0)
-    pat = pl.pallas_call(
+    pat_early, pat_late = pl.pallas_call(
         patch_kernel,
-        out_shape=jax.ShapeDtypeStruct((PS, CH, 16, AUG * SIDE), jnp.bfloat16),
+        out_shape=(
+            jax.ShapeDtypeStruct((PS, CH, 16, EARLY * SIDE), jnp.bfloat16),
+            jax.ShapeDtypeStruct((PS, CH, 16, (GRID - EARLY) * SIDE), jnp.bfloat16),
+        ),
         in_specs=[SMEM, SMEM, VMEM],
-        out_specs=VMEM,
+        out_specs=(VMEM, VMEM),
         scratch_shapes=[
             pltpu.VMEM((SIDE, AUG * SIDE), jnp.bfloat16),
             pltpu.VMEM((CH, 2 * AUG, PITCH, LANES), jnp.float32),
-            pltpu.VMEM((PS, 16, SIDE), jnp.float32),
         ],
-        compiler_params=pltpu.CompilerParams(vmem_limit_bytes=28 * MIB),
+        compiler_params=pltpu.CompilerParams(vmem_limit_bytes=20 * MIB),
         cost_estimate=pl.CostEstimate(
             flops=20_000_000_000, bytes_accessed=20_000_000, transcendentals=0
         ),
@@ -230,17 +240,17 @@
     parts = pl.pallas_call(
         gradient_kernel,
         out_shape=jax.ShapeDtypeStruct((AUG, MROWS, LANES), jnp.int16),
-        in_specs=[pl.BlockSpec(memory_space=pl.ANY), VMEM],
+        in_specs=[VMEM, pl.BlockSpec(memory_space=pl.ANY), VMEM],
         out_specs=VMEM,
         scratch_shapes=[
-            pltpu.VMEM((PS, CH, 16, AUG * SIDE), jnp.bfloat16),
+            pltpu.VMEM((PS, CH, 16, (GRID - EARLY) * SIDE), jnp.bfloat16),
             pltpu.VMEM((AUG * SIDE, COLS), jnp.bfloat16),
             pltpu.VMEM((PATCH + 12, LANES), jnp.float32),
             pltpu.SemaphoreType.DMA,
         ],
         compiler_params=pltpu.CompilerParams(vmem_limit_bytes=48 * MIB),
-    )(pat, blocks)
-    parts = lax.all_to_all(parts, "aug", 0, 0)
+    )(pat_early, pat_late, blocks)
+    parts = lax.all_to_all(parts, "aug", 0, 0, axis_index_groups=[ORDER])
     chunks = jax.ShapeDtypeStruct((images_in_all, 16, LANES), jnp.int16)
     term, norm = pl.pallas_call(
         shard_kernel,

time: 93 us -> 93.5 us (level)
  the two profiles are of different devices: /device:TPU:1 before, /device:TPU:8 now
where the time goes in v4:
time: 93.5 us; the launch traced here: 93 us
  waiting for transfers between devices  29.1 us (31%)
  blocking collectives  21.8 us (23%)
  starting transfers between devices  19.8 us (21%)
  Pallas kernels  14.3 us (15%)
  local copies, waits for them, and re-layouts  5.42 us (6%)
  other arithmetic  1.78 us (2%)
    all_to_all x1, blocking collectives, per_device(): pieces = lax.all_to_all(term, 'dp', 0, 0)  21.8 us
    all_to_all x1, waiting for transfers between devices, per_device(): gathered = lax.all_to_all(spread, 'dp', 0, 0)  10 us
    all_to_all x1, waiting for transfers between devices, per_device(): parts = lax.all_to_all(parts, 'aug', 0, 0, axis_index_groups=[ORDER])  9.62 us
    all_to_all x1, waiting for transfers between devices, per_device(): blocks = lax.all_to_all(blocks, 'aug', 0, 0)  9.48 us
    all_to_all x1, starting transfers between devices, per_device(): blocks = lax.all_to_all(blocks, 'aug', 0, 0)  9.24 us
    pallas_call x1, Pallas kernels, per_device(): pl.pallas_call(patch_kernel, out_shape=(jax.ShapeDtypeStruct((PS, CH, 16,...  8.36 us
    all_to_all x1, starting transfers between devices, per_device(): parts = lax.all_to_all(parts, 'aug', 0, 0, axis_index_groups=[ORDER])  6.75 us
    pallas_call x1, Pallas kernels, per_device(): pl.pallas_call(gradient_kernel, out_shape=jax.ShapeDtypeStruct((AUG, MROW...  4.75 us
  transfers between devices with their start and end apart: 3, of which 3 were waited for; matrix products, arithmetic and copies ran while one was open for 1% of the time, Pallas kernels for 9%

profile of v4, /device:TPU:8, one launch (start us, length us, event | category | flops | bytes accessed | tf_op | source)
XLA Modules:
  0.0 93.0 jit_solution(2626748744464416132)
XLA Ops:
  0.6 0.0 copy-start.4
  0.6 0.0 copy-start.2
  0.7 2.2 %copy.10 = bf16[1664,256]{1,0:T(8,128)(2,1)} copy(bf16[1664,256]{0,1:T(8,128)(2,1)} %bitcast.13) | data formatting | bytes 1703936 | tf_op jit(solution)/shard_map/transpose | solution.py:221
  2.9 9.2 %all-to-all-start = ((bf16[16,104,256]{2,1,0:T(8,128)(2,1)}), bf16[16,104,256]{2,1,0:T(8,128)(2,1)S(1)}, u32[]{:S(2)}, u32[]{:S(2)}) async-start(bf16[16,104,256]{2,1,0:T(8,128)(2,1)} %bitcast.6), calls=%async_computation | async-start | bytes 1703936 | tf_op jit(solution)/shard_map/all_to_all | solution.py:222
  12.1 0.0 copy-done.4
  12.1 0.1 copy.9.offs
  12.2 0.0 copy-done.2
  12.2 0.0 copy-start.1
  12.2 1.0 %copy-done.1 = bf16[1,3,256,256]{3,2,1,0:T(8,128)(2,1)S(1)} copy-done((bf16[1,3,256,256]{3,2,1,0:T(8,128)(2,1)S(1)}, bf16[1,3,256,256]{3,2,1,0:T(8,128)(2,1)}, u32[]{:S(2)}) %copy-start.1) | copy-done | bytes 393240
  13.2 8.4 %shard_map.85 = (bf16[14,3,16,1792]{3,2,1,0:T(8,128)(2,1)S(1)}, bf16[14,3,16,2304]{3,2,1,0:T(8,128)(2,1)S(1)}) custom-call(s32[16,2]{1,0:T(8,128)S(1)} %copy.9.offs, s32[16]{0:T(128)S(1)} %bitcast.12, bf16[3,256,256]{2,1,0:T(8,128)(2,1)S(1)} %bitcast.11), custom_call_target="tpu_custom_call" | custom-call | flops 20000000000 | bytes 20000000 | tf_op jit(solution)/shard_map/pallas_call | solution.py:223
  21.6 0.0 copy-start
  21.6 1.6 %copy-done = bf16[14,3,16,2304]{3,2,1,0:T(8,128)(2,1)} copy-done((bf16[14,3,16,2304]{3,2,1,0:T(8,128)(2,1)}, bf16[14,3,16,2304]{3,2,1,0:T(8,128)(2,1)S(1)}, u32[]{:S(2)}) %copy-start) | copy-done | bytes 3096600
  23.2 9.5 %all-to-all-done.grads = bf16[16,104,256]{2,1,0:T(8,128)(2,1)S(1)} async-done(((bf16[16,104,256]{2,1,0:T(8,128)(2,1)}), bf16[16,104,256]{2,1,0:T(8,128)(2,1)S(1)}, u32[]{:S(2)}, u32[]{:S(2)}) %all-to-all-start) | async-done | bytes 852000 | tf_op jit(solution)/shard_map/all_to_all | solution.py:222
  32.6 0.0 copy-start.3
  32.6 4.8 %shard_map.86 = s16[16,48,128]{2,1,0:T(8,128)(2,1)} custom-call(bf16[14,3,16,1792]{3,2,1,0:T(8,128)(2,1)S(1)} %get-tuple-element.7.pat_early, bf16[14,3,16,2304]{3,2,1,0:T(8,128)(2,1)} %copy-done, bf16[16,104,256]{2,1,0:T(8,128)(2,1)S(1)} %all-to-all-done.grads), custom_call_target="tpu_custom_call" | custom-call | tf_op jit(solution)/shard_map/pallas_call | solution.py:240
  37.4 6.7 %all-to-all-start.1 = ((s16[16,48,128]{2,1,0:T(8,128)(2,1)}), s16[16,48,128]{2,1,0:T(8,128)(2,1)S(1)}, u32[]{:S(2)}, u32[]{:S(2)}) async-start(s16[16,48,128]{2,1,0:T(8,128)(2,1)} %shard_map.86), calls=%async_computation.1 | async-start | bytes 393216 | tf_op jit(solution)/shard_map/all_to_all | solution.py:253
  44.2 9.6 %all-to-all-done.1.parts = s16[16,48,128]{2,1,0:T(8,128)(2,1)S(1)} async-done(((s16[16,48,128]{2,1,0:T(8,128)(2,1)}), s16[16,48,128]{2,1,0:T(8,128)(2,1)S(1)}, u32[]{:S(2)}, u32[]{:S(2)}) %all-to-all-start.1) | async-done | bytes 196640 | tf_op jit(solution)/shard_map/all_to_all | solution.py:253
  53.8 0.4 shard_map.87
  54.2 21.8 %all_to_all.20.pieces = s16[32,16,128]{2,1,0:T(8,128)(2,1)S(1)} all-to-all(s16[32,16,128]{2,1,0:T(8,128)(2,1)S(1)} %get-tuple-element.9), channel_id=1, replica_groups=mesh['dp'=32,'aug'=16] {'dp'}, dimensions={0} | all-to-all | bytes 262144 | tf_op jit(solution)/shard_map/all_to_all | solution.py:266
  76.0 0.8 shard_map.88
  76.8 3.9 %all-to-all-start.3 = ((s16[32,16,128]{2,1,0:T(8,128)(2,1)}), s16[32,16,128]{2,1,0:T(8,128)(2,1)S(1)}, u32[]{:S(2)}, u32[]{:S(2)}) async-start(s16[32,16,128]{2,1,0:T(8,128)(2,1)} %shard_map.88), calls=%async_computation.3 | async-start | bytes 262144 | tf_op jit(solution)/shard_map/all_to_all | solution.py:274
  80.6 0.5 slice.7
  81.1 10.0 %all-to-all-done.3.chunks = s16[32,16,128]{2,1,0:T(8,128)(2,1)S(1)} async-done(((s16[32,16,128]{2,1,0:T(8,128)(2,1)}), s16[32,16,128]{2,1,0:T(8,128)(2,1)S(1)}, u32[]{:S(2)}, u32[]{:S(2)}) %all-to-all-start.3) | async-done | bytes 131104 | tf_op jit(solution)/shard_map/all_to_all | solution.py:274
  91.2 0.1 shard_map.89
  91.2 0.0 copy-done.3
  91.2 1.8 %slice_multiply_fusion = (f32[61152]{0:T(1024)}, f32[61152]{0:T(1024)}) fusion(f32[61440]{0:T(1024)S(1)} %bitcast.10, f32[61152]{0:T(1024)S(1)} %copy-done.3, f32[61152]{0:T(1024)} %param.11), kind=kLoop, calls=%fused_computation.1 | loop fusion | flops 305760 | bytes 1223040 | tf_op jit(solution)/shard_map/div | solution.py:283
Async XLA Ops:
  0.6 11.5 %copy-start.4 = (s32[1,16,2]{1,2,0:T(2,128)S(1)}, s32[1,16,2]{1,2,0:T(2,128)}, u32[]{:S(2)}) copy-start(s32[1,16,2]{1,2,0:T(2,128)} %param.7) | copy-start | bytes 388
  0.6 11.5 %copy-start.2 = (s32[1,16]{1,0:T(1,128)S(1)}, s32[1,16]{1,0:T(1,128)}, u32[]{:S(2)}) copy-start(s32[1,16]{1,0:T(1,128)} %param.8) | copy-start | bytes 196
  2.9 29.8 %all-to-all-start = ((bf16[16,104,256]{2,1,0:T(8,128)(2,1)}), bf16[16,104,256]{2,1,0:T(8,128)(2,1)S(1)}, u32[]{:S(2)}, u32[]{:S(2)}) async-start(bf16[16,104,256]{2,1,0:T(8,128)(2,1)} %bitcast.6), calls=%async_computation | async-start | bytes 1703936 | tf_op jit(solution)/shard_map/all_to_all | solution.py:222
  12.2 1.0 %copy-start.1 = (bf16[1,3,256,256]{3,2,1,0:T(8,128)(2,1)S(1)}, bf16[1,3,256,256]{3,2,1,0:T(8,128)(2,1)}, u32[]{:S(2)}) copy-start(bf16[1,3,256,256]{3,2,1,0:T(8,128)(2,1)} %param.6) | copy-start | bytes 1179652
  21.6 1.6 %copy-start = (bf16[14,3,16,2304]{3,2,1,0:T(8,128)(2,1)}, bf16[14,3,16,2304]{3,2,1,0:T(8,128)(2,1)S(1)}, u32[]{:S(2)}) copy-start(bf16[14,3,16,2304]{3,2,1,0:T(8,128)(2,1)S(1)} %get-tuple-element.8.pat_late) | copy-start | bytes 9289732
  32.6 58.6 %copy-start.3 = (f32[61152]{0:T(1024)S(1)}, f32[61152]{0:T(1024)}, u32[]{:S(2)}) copy-start(f32[61152]{0:T(1024)} %param.10) | copy-start | bytes 733828
  37.4 16.4 %all-to-all-start.1 = ((s16[16,48,128]{2,1,0:T(8,128)(2,1)}), s16[16,48,128]{2,1,0:T(8,128)(2,1)S(1)}, u32[]{:S(2)}, u32[]{:S(2)}) async-start(s16[16,48,128]{2,1,0:T(8,128)(2,1)} %shard_map.86), calls=%async_computation.1 | async-start | bytes 393216 | tf_op jit(solution)/shard_map/all_to_all | solution.py:253
  76.8 14.4 %all-to-all-start.3 = ((s16[32,16,128]{2,1,0:T(8,128)(2,1)}), s16[32,16,128]{2,1,0:T(8,128)(2,1)S(1)}, u32[]{:S(2)}, u32[]{:S(2)}) async-start(s16[32,16,128]{2,1,0:T(8,128)(2,1)} %shard_map.88), calls=%async_computation.3 | async-start | bytes 262144 | tf_op jit(solution)/shard_map/all_to_all | solution.py:274

commit v5 on v4

--- a/solution.py
+++ b/solution.py
@@ -21,7 +21,8 @@
 CLIP = math.sqrt(PATCH * D)
 SHARD = PATCH * D // AUG
 SROWS = 38
-MROWS = 48
+MROWS = 32
+HELD = 40
 PROWS = 15
 ROWS = 480
 FULL = 32700.0
@@ -30,7 +31,7 @@
 FINE = 1e6
 SPARE = 8
 MIB = 1024 * 1024
-EARLY = 7
+EARLY = 6
 ORDER = list(range(0, AUG, 2)) + list(range(1, AUG, 2))
 PITCH = SIDE + SPARE
 
@@ -95,7 +96,7 @@
         lax.fori_loop(0, CH * count, functools.partial(assemble, pat, begin, count), 0)
 
 
-def gradient_kernel(pat_early, pat_late, grads, msg, near, gord, flat, sem):
+def gradient_kernel(pat_early, pat_late, grads, msg, near, gord, flat, strip, sem):
     fetch = pltpu.make_async_copy(pat_late, near, sem)
     fetch.start()
     flat[...] = jnp.zeros(flat.shape, jnp.float32)
@@ -123,15 +124,33 @@
     squares = jnp.full((1, LANES), jnp.sum(values * values), jnp.float32)
     coarse = jnp.floor(jnp.log(jnp.maximum(squares, 1e-36)) * COARSE)
     fine = (squares / jnp.exp(coarse / COARSE) - 1.0) * FINE
-    row = lax.broadcasted_iota(jnp.int32, (MROWS, LANES), 0)
-    inside = (row < SROWS) & (lax.broadcasted_iota(jnp.int32, (MROWS, LANES), 1) < COLS)
-    tail = jnp.where(row == SROWS + 1, coarse, jnp.where(row == SROWS + 2, rounded(fine), 0.0))
+    row = lax.broadcasted_iota(jnp.int32, (HELD, LANES), 0)
+    lane = lax.broadcasted_iota(jnp.int32, (HELD, LANES), 1)
+    inside = (row < SROWS) & (lane < COLS)
+    tail = jnp.where(lane < COLS, coarse, rounded(fine))
     for order, b in enumerate(ORDER):
         first = 147 * b // 4
-        block = jnp.where(inside, flat[first:first + MROWS, :], 0.0)
+        block = jnp.where(inside, flat[first:first + HELD, :], 0.0)
         codes, level = encode(block, jnp.abs(block))
         codes = jnp.where(row < SROWS, codes, jnp.where(row == SROWS, level, tail))
-        msg[order] = codes.astype(jnp.int32).astype(jnp.int16)
+        over = codes[MROWS:]
+        for q in range(4):
+            strip[7 * q:7 * q + 8, :] = pltpu.roll(over, COLS - 24 * q, 1)
+        upper, lower = pltpu.roll(over, 8, 1)[0:4], pltpu.roll(over, 16, 1)[4:8]
+        strip[28:32, :] = jnp.where(lane[0:4] < COLS + 8, upper, lower)
+        packed = jnp.where(lane[0:MROWS] < COLS, codes[0:MROWS], strip[...])
+        msg[order] = packed.astype(jnp.int32).astype(jnp.int16)
+
+
+def unpacked(part):
+    row = lax.broadcasted_iota(jnp.int32, (8, LANES), 0)
+    lane = lax.broadcasted_iota(jnp.int32, (8, LANES), 1)
+    upper = pltpu.roll(pltpu.roll(part[24:32], LANES - 8, 1), 4, 0)
+    over = jnp.where(row < 4, upper, pltpu.roll(part[24:32], LANES - 16, 1))
+    for q in range(4):
+        piece = pltpu.roll(part[7 * q:7 * q + 8], LANES - COLS + 24 * q, 1)
+        over = jnp.where((lane >= 24 * q) & (lane < 24 * q + 24), piece, over)
+    return over
 
 
 def rounded(value):
@@ -153,12 +172,14 @@
 
 
 def shard_kernel(index, parts, term, norm, lined, even):
-    squares = jnp.zeros((1, LANES), jnp.float32)
+    squares = jnp.zeros((1, 1), jnp.float32)
     opened = []
     for a in range(AUG):
         part = plain(parts[ORDER.index(a)])
-        opened.append(part[0:SROWS] * step_of(part[SROWS:SROWS + 1]))
-        coarse, fine = part[SROWS + 1:SROWS + 2], part[SROWS + 2:SROWS + 3]
+        over = unpacked(part)
+        step = step_of(over[6:7])
+        opened.append(jnp.concatenate([part * step, over * step])[0:SROWS])
+        coarse, fine = over[7:8, COLS - 8:COLS - 7], over[7:8, COLS:COLS + 1]
         squares = squares + jnp.exp(coarse / COARSE) * (1.0 + fine / FINE)
     length = jnp.sqrt(squares / (AUG * AUG) + 1e-6)
     norm[...] = jnp.broadcast_to(length, (8, LANES))
@@ -246,6 +267,7 @@
             pltpu.VMEM((PS, CH, 16, (GRID - EARLY) * SIDE), jnp.bfloat16),
             pltpu.VMEM((AUG * SIDE, COLS), jnp.bfloat16),
             pltpu.VMEM((PATCH + 12, LANES), jnp.float32),
+            pltpu.VMEM((MROWS, LANES), jnp.float32),
             pltpu.SemaphoreType.DMA,
         ],
         compiler_params=pltpu.CompilerParams(vmem_limit_bytes=48 * MIB),

time: 93.5 us -> 91.6 us (0.980)
  waiting for transfers between devices: 29.1 us -> 26.3 us
  local copies, waits for them, and re-layouts: 5.42 us -> 6.89 us
  other arithmetic: 1.78 us -> 0.83 us
    all_to_all x1, waiting for transfers between devices: 9.62 us -> 8.22 us  [per_device(): parts = lax.all_to_all(parts, 'aug', 0, 0, axis_index_groups=[ORDER])]
    all_to_all x1, waiting for transfers between devices: 9.48 us -> 8.08 us  [per_device(): blocks = lax.all_to_all(blocks, 'aug', 0, 0)]
    div x1, other arithmetic: 1.78 us -> 0.83 us  [per_device(): clipped_mean = clipped_sum / images_in_all]
where the time goes in v5:
time: 91.6 us; the launch traced here: 91.2 us
  waiting for transfers between devices  26.3 us (29%)
  blocking collectives  21.8 us (24%)
  starting transfers between devices  19.8 us (22%)
  Pallas kernels  14.8 us (16%)
  local copies, waits for them, and re-layouts  6.89 us (8%)
    all_to_all x1, blocking collectives, per_device(): pieces = lax.all_to_all(term, 'dp', 0, 0)  21.8 us
    all_to_all x1, waiting for transfers between devices, per_device(): gathered = lax.all_to_all(spread, 'dp', 0, 0)  10 us
    all_to_all x1, starting transfers between devices, per_device(): blocks = lax.all_to_all(blocks, 'aug', 0, 0)  9.24 us
    pallas_call x1, Pallas kernels, per_device(): pl.pallas_call(patch_kernel, out_shape=(jax.ShapeDtypeStruct((PS, CH, 16,...  8.33 us
    all_to_all x1, waiting for transfers between devices, per_device(): parts = lax.all_to_all(parts, 'aug', 0, 0, axis_index_groups=[ORDER])  8.22 us
    all_to_all x1, waiting for transfers between devices, per_device(): blocks = lax.all_to_all(blocks, 'aug', 0, 0)  8.08 us
    all_to_all x1, starting transfers between devices, per_device(): parts = lax.all_to_all(parts, 'aug', 0, 0, axis_index_groups=[ORDER])  6.74 us
    pallas_call x1, Pallas kernels, per_device(): pl.pallas_call(gradient_kernel, out_shape=jax.ShapeDtypeStruct((AUG, MROW...  4.98 us
  transfers between devices with their start and end apart: 3, of which 3 were waited for; matrix products, arithmetic and copies ran while one was open for 1% of the time, Pallas kernels for 9%

profile of v5, /device:TPU:8, one launch (start us, length us, event | category | flops | bytes accessed | tf_op | source)
XLA Modules:
  0.0 91.2 jit_solution(15023562480985828232)
XLA Ops:
  0.6 2.2 %copy.10 = bf16[1664,256]{1,0:T(8,128)(2,1)} copy(bf16[1664,256]{0,1:T(8,128)(2,1)} %bitcast.13) | data formatting | bytes 1703936 | tf_op jit(solution)/shard_map/transpose | solution.py:242
  2.9 9.2 %all-to-all-start = ((bf16[16,104,256]{2,1,0:T(8,128)(2,1)}), bf16[16,104,256]{2,1,0:T(8,128)(2,1)S(1)}, u32[]{:S(2)}, u32[]{:S(2)}) async-start(bf16[16,104,256]{2,1,0:T(8,128)(2,1)} %bitcast.6), calls=%async_computation | async-start | bytes 1703936 | tf_op jit(solution)/shard_map/all_to_all | solution.py:243
  12.1 0.8 copy.9.offs
  12.9 0.0 copy-start.1
  12.9 1.0 %copy-done.1 = bf16[1,3,256,256]{3,2,1,0:T(8,128)(2,1)S(1)} copy-done((bf16[1,3,256,256]{3,2,1,0:T(8,128)(2,1)S(1)}, bf16[1,3,256,256]{3,2,1,0:T(8,128)(2,1)}, u32[]{:S(2)}) %copy-start.1) | copy-done | bytes 393240
  13.9 0.0 copy-start.2
  13.9 0.7 copy-done.2
  14.5 8.3 %shard_map.85 = (bf16[14,3,16,1536]{3,2,1,0:T(8,128)(2,1)S(1)}, bf16[14,3,16,2560]{3,2,1,0:T(8,128)(2,1)S(1)}) custom-call(s32[16,2]{1,0:T(8,128)S(1)} %copy.9.offs, s32[16]{0:T(128)S(1)} %bitcast.12, bf16[3,256,256]{2,1,0:T(8,128)(2,1)S(1)} %bitcast.11), custom_call_target="tpu_custom_call" | custom-call | flops 20000000000 | bytes 20000000 | tf_op jit(solution)/shard_map/pallas_call | solution.py:244
  22.9 0.0 copy-start
  22.9 1.7 %copy-done = bf16[14,3,16,2560]{3,2,1,0:T(8,128)(2,1)} copy-done((bf16[14,3,16,2560]{3,2,1,0:T(8,128)(2,1)}, bf16[14,3,16,2560]{3,2,1,0:T(8,128)(2,1)S(1)}, u32[]{:S(2)}) %copy-start) | copy-done | bytes 3440664
  24.6 8.1 %all-to-all-done.grads = bf16[16,104,256]{2,1,0:T(8,128)(2,1)S(1)} async-done(((bf16[16,104,256]{2,1,0:T(8,128)(2,1)}), bf16[16,104,256]{2,1,0:T(8,128)(2,1)S(1)}, u32[]{:S(2)}, u32[]{:S(2)}) %all-to-all-start) | async-done | bytes 852000 | tf_op jit(solution)/shard_map/all_to_all | solution.py:243
  32.7 0.0 copy-start.3
  32.7 0.0 copy-start.4
  32.7 5.0 %shard_map.86 = s16[16,32,128]{2,1,0:T(8,128)(2,1)} custom-call(bf16[14,3,16,1536]{3,2,1,0:T(8,128)(2,1)S(1)} %get-tuple-element.7.pat_early, bf16[14,3,16,2560]{3,2,1,0:T(8,128)(2,1)} %copy-done, bf16[16,104,256]{2,1,0:T(8,128)(2,1)S(1)} %all-to-all-done.grads), custom_call_target="tpu_custom_call" | custom-call | tf_op jit(solution)/shard_map/pallas_call | solution.py:261
  37.7 6.7 %all-to-all-start.1 = ((s16[16,32,128]{2,1,0:T(8,128)(2,1)}), s16[16,32,128]{2,1,0:T(8,128)(2,1)S(1)}, u32[]{:S(2)}, u32[]{:S(2)}) async-start(s16[16,32,128]{2,1,0:T(8,128)(2,1)} %shard_map.86), calls=%async_computation.1 | async-start | bytes 262144 | tf_op jit(solution)/shard_map/all_to_all | solution.py:275
  44.4 8.2 %all-to-all-done.1.parts = s16[16,32,128]{2,1,0:T(8,128)(2,1)S(1)} async-done(((s16[16,32,128]{2,1,0:T(8,128)(2,1)}), s16[16,32,128]{2,1,0:T(8,128)(2,1)S(1)}, u32[]{:S(2)}, u32[]{:S(2)}) %all-to-all-start.1) | async-done | bytes 131104 | tf_op jit(solution)/shard_map/all_to_all | solution.py:275
  52.6 0.6 shard_map.87
  53.3 21.8 %all_to_all.20.pieces = s16[32,16,128]{2,1,0:T(8,128)(2,1)S(1)} all-to-all(s16[32,16,128]{2,1,0:T(8,128)(2,1)S(1)} %get-tuple-element.9), channel_id=1, replica_groups=mesh['dp'=32,'aug'=16] {'dp'}, dimensions={0} | all-to-all | bytes 262144 | tf_op jit(solution)/shard_map/all_to_all | solution.py:288
  75.1 0.8 shard_map.88
  75.8 3.9 %all-to-all-start.3 = ((s16[32,16,128]{2,1,0:T(8,128)(2,1)}), s16[32,16,128]{2,1,0:T(8,128)(2,1)S(1)}, u32[]{:S(2)}, u32[]{:S(2)}) async-start(s16[32,16,128]{2,1,0:T(8,128)(2,1)} %shard_map.88), calls=%async_computation.3 | async-start | bytes 262144 | tf_op jit(solution)/shard_map/all_to_all | solution.py:296
  79.7 0.5 slice.7
  80.2 10.0 %all-to-all-done.3.chunks = s16[32,16,128]{2,1,0:T(8,128)(2,1)S(1)} async-done(((s16[32,16,128]{2,1,0:T(8,128)(2,1)}), s16[32,16,128]{2,1,0:T(8,128)(2,1)S(1)}, u32[]{:S(2)}, u32[]{:S(2)}) %all-to-all-start.3) | async-done | bytes 131104 | tf_op jit(solution)/shard_map/all_to_all | solution.py:296
  90.3 0.1 shard_map.89
  90.3 0.0 copy-done.3
  90.3 0.0 copy-done.4
  90.3 0.8 slice_multiply_fusion
Async XLA Ops:
  2.9 29.8 %all-to-all-start = ((bf16[16,104,256]{2,1,0:T(8,128)(2,1)}), bf16[16,104,256]{2,1,0:T(8,128)(2,1)S(1)}, u32[]{:S(2)}, u32[]{:S(2)}) async-start(bf16[16,104,256]{2,1,0:T(8,128)(2,1)} %bitcast.6), calls=%async_computation | async-start | bytes 1703936 | tf_op jit(solution)/shard_map/all_to_all | solution.py:243
  12.9 1.0 %copy-start.1 = (bf16[1,3,256,256]{3,2,1,0:T(8,128)(2,1)S(1)}, bf16[1,3,256,256]{3,2,1,0:T(8,128)(2,1)}, u32[]{:S(2)}) copy-start(bf16[1,3,256,256]{3,2,1,0:T(8,128)(2,1)} %param.6) | copy-start | bytes 1179652
  13.9 0.7 copy-start.2
  22.9 1.7 %copy-start = (bf16[14,3,16,2560]{3,2,1,0:T(8,128)(2,1)}, bf16[14,3,16,2560]{3,2,1,0:T(8,128)(2,1)S(1)}, u32[]{:S(2)}) copy-start(bf16[14,3,16,2560]{3,2,1,0:T(8,128)(2,1)S(1)} %get-tuple-element.8.pat_late) | copy-start | bytes 10321924
  32.7 57.7 %copy-start.3 = (f32[61152]{0:T(1024)S(1)}, f32[61152]{0:T(1024)}, u32[]{:S(2)}) copy-start(f32[61152]{0:T(1024)} %param.10) | copy-start | bytes 733828
  32.7 57.7 %copy-start.4 = (f32[61152]{0:T(1024)S(1)}, f32[61152]{0:T(1024)}, u32[]{:S(2)}) copy-start(f32[61152]{0:T(1024)} %param.11) | copy-start | bytes 733828
  37.7 15.0 %all-to-all-start.1 = ((s16[16,32,128]{2,1,0:T(8,128)(2,1)}), s16[16,32,128]{2,1,0:T(8,128)(2,1)S(1)}, u32[]{:S(2)}, u32[]{:S(2)}) async-start(s16[16,32,128]{2,1,0:T(8,128)(2,1)} %shard_map.86), calls=%async_computation.1 | async-start | bytes 262144 | tf_op jit(solution)/shard_map/all_to_all | solution.py:275
  75.8 14.4 %all-to-all-start.3 = ((s16[32,16,128]{2,1,0:T(8,128)(2,1)}), s16[32,16,128]{2,1,0:T(8,128)(2,1)S(1)}, u32[]{:S(2)}, u32[]{:S(2)}) async-start(s16[32,16,128]{2,1,0:T(8,128)(2,1)} %shard_map.88), calls=%async_computation.3 | async-start | bytes 262144 | tf_op jit(solution)/shard_map/all_to_all | solution.py:296

commit v6 on v5

--- a/solution.py
+++ b/solution.py
@@ -96,25 +96,48 @@
         lax.fori_loop(0, CH * count, functools.partial(assemble, pat, begin, count), 0)
 
 
-def gradient_kernel(pat_early, pat_late, grads, msg, near, gord, flat, strip, sem):
-    fetch = pltpu.make_async_copy(pat_late, near, sem)
-    fetch.start()
-    flat[...] = jnp.zeros(flat.shape, jnp.float32)
-    for k in range(AUG):
+def gradient_kernel(
+    pat_early, pat_late, grads, msg, near, gord, flat, strip, total, sems
+):
+    late = near.shape[3] // 2
+    fetches = []
+    for half in range(2):
+        part = pl.ds(half * late, late)
+        fetches.append(
+            pltpu.make_async_copy(
+                pat_late.at[:, :, :, part], near.at[:, :, :, part], sems.at[half]
+            )
+        )
+        fetches[half].start()
+
+    def turn(k, carry):
         turned = grads[k].T
         for y in range(GRID):
-            gord[(y * AUG + k) * 16:(y * AUG + k + 1) * 16, :] = turned[y * 16:(y + 1) * 16, :]
-    total = jnp.dot(
-        pat_early[...].reshape(PS * CH * 16, EARLY * SIDE),
-        gord[0:EARLY * SIDE, :],
-        preferred_element_type=jnp.float32,
-    )
-    fetch.wait()
-    total = total + jnp.dot(
-        near[...].reshape(PS * CH * 16, (GRID - EARLY) * SIDE),
-        gord[EARLY * SIDE:, :],
-        preferred_element_type=jnp.float32,
-    )
+            place = pl.ds(pl.multiple_of(y * AUG * 16 + k * 16, 16), 16)
+            gord[place, :] = turned[y * 16:(y + 1) * 16, :]
+        return carry
+
+    def multiply(source, begin, end, first):
+        def part(step, carry):
+            many = PS // 2 * CH * 16
+            left = source[pl.ds(step * (PS // 2), PS // 2), :, :, begin:end]
+            value = jnp.dot(
+                left.reshape(many, end - begin),
+                gord[first:first + end - begin, :],
+                preferred_element_type=jnp.float32,
+            )
+            rows = pl.ds(pl.multiple_of(step * many, 16), many)
+            total[rows, :] = value if first == 0 else total[rows, :] + value
+            return carry
+
+        lax.fori_loop(0, 2, part, 0)
+
+    flat[PATCH:, :] = jnp.zeros((12, LANES), jnp.float32)
+    [turn(k, 0) for k in range(AUG)]
+    multiply(pat_early, 0, EARLY * SIDE, 0)
+    for half in range(2):
+        fetches[half].wait()
+        multiply(near, half * late, (half + 1) * late, EARLY * SIDE + half * late)
     for v in range(PS):
         for c in range(CH):
             first = v * CH * 16 + c * 16
@@ -268,7 +291,8 @@
             pltpu.VMEM((AUG * SIDE, COLS), jnp.bfloat16),
             pltpu.VMEM((PATCH + 12, LANES), jnp.float32),
             pltpu.VMEM((MROWS, LANES), jnp.float32),
-            pltpu.SemaphoreType.DMA,
+            pltpu.VMEM((PS * CH * 16, COLS), jnp.float32),
+            pltpu.SemaphoreType.DMA((2,)),
         ],
         compiler_params=pltpu.CompilerParams(vmem_limit_bytes=48 * MIB),
     )(pat_early, pat_late, blocks)

time: 91.6 us -> 91.1 us (level)
  no operation moved by 1% of the time
where the time goes in v6:
time: 91.1 us; the launch traced here: 90.7 us
  waiting for transfers between devices  26.3 us (29%)
  blocking collectives  21.8 us (24%)
  starting transfers between devices  19.8 us (22%)
  Pallas kernels  14.3 us (16%)
  local copies, waits for them, and re-layouts  6.89 us (8%)
    all_to_all x1, blocking collectives, per_device(): pieces = lax.all_to_all(term, 'dp', 0, 0)  21.8 us
    all_to_all x1, waiting for transfers between devices, per_device(): gathered = lax.all_to_all(spread, 'dp', 0, 0)  10 us
    all_to_all x1, starting transfers between devices, per_device(): blocks = lax.all_to_all(blocks, 'aug', 0, 0)  9.24 us
    pallas_call x1, Pallas kernels, per_device(): pl.pallas_call(patch_kernel, out_shape=(jax.ShapeDtypeStruct((PS, CH, 16,...  8.37 us
    all_to_all x1, waiting for transfers between devices, per_device(): parts = lax.all_to_all(parts, 'aug', 0, 0, axis_index_groups=[ORDER])  8.22 us
    all_to_all x1, waiting for transfers between devices, per_device(): blocks = lax.all_to_all(blocks, 'aug', 0, 0)  8.03 us
    all_to_all x1, starting transfers between devices, per_device(): parts = lax.all_to_all(parts, 'aug', 0, 0, axis_index_groups=[ORDER])  6.75 us
    pallas_call x1, Pallas kernels, per_device(): pl.pallas_call(gradient_kernel, out_shape=jax.ShapeDtypeStruct((AUG, MROW...  4.46 us
  transfers between devices with their start and end apart: 3, of which 3 were waited for; matrix products, arithmetic and copies ran while one was open for 1% of the time, Pallas kernels for 9%

profile of v6, /device:TPU:8, one launch (start us, length us, event | category | flops | bytes accessed | tf_op | source)
XLA Modules:
  0.0 90.7 jit_solution(7114637009714948726)
XLA Ops:
  0.6 2.2 %copy.10 = bf16[1664,256]{1,0:T(8,128)(2,1)} copy(bf16[1664,256]{0,1:T(8,128)(2,1)} %bitcast.13) | data formatting | bytes 1703936 | tf_op jit(solution)/shard_map/transpose | solution.py:265
  2.9 9.2 %all-to-all-start = ((bf16[16,104,256]{2,1,0:T(8,128)(2,1)}), bf16[16,104,256]{2,1,0:T(8,128)(2,1)S(1)}, u32[]{:S(2)}, u32[]{:S(2)}) async-start(bf16[16,104,256]{2,1,0:T(8,128)(2,1)} %bitcast.6), calls=%async_computation | async-start | bytes 1703936 | tf_op jit(solution)/shard_map/all_to_all | solution.py:266
  12.1 0.8 copy.9.offs
  12.9 0.0 copy-start.1
  12.9 1.0 %copy-done.1 = bf16[1,3,256,256]{3,2,1,0:T(8,128)(2,1)S(1)} copy-done((bf16[1,3,256,256]{3,2,1,0:T(8,128)(2,1)S(1)}, bf16[1,3,256,256]{3,2,1,0:T(8,128)(2,1)}, u32[]{:S(2)}) %copy-start.1) | copy-done | bytes 393240
  13.9 0.0 copy-start.2
  13.9 0.7 copy-done.2
  14.5 8.4 %shard_map.85 = (bf16[14,3,16,1536]{3,2,1,0:T(8,128)(2,1)S(1)}, bf16[14,3,16,2560]{3,2,1,0:T(8,128)(2,1)S(1)}) custom-call(s32[16,2]{1,0:T(8,128)S(1)} %copy.9.offs, s32[16]{0:T(128)S(1)} %bitcast.12, bf16[3,256,256]{2,1,0:T(8,128)(2,1)S(1)} %bitcast.11), custom_call_target="tpu_custom_call" | custom-call | flops 20000000000 | bytes 20000000 | tf_op jit(solution)/shard_map/pallas_call | solution.py:267
  22.9 0.0 copy-start
  22.9 1.7 %copy-done = bf16[14,3,16,2560]{3,2,1,0:T(8,128)(2,1)} copy-done((bf16[14,3,16,2560]{3,2,1,0:T(8,128)(2,1)}, bf16[14,3,16,2560]{3,2,1,0:T(8,128)(2,1)S(1)}, u32[]{:S(2)}) %copy-start) | copy-done | bytes 3440664
  24.6 8.0 %all-to-all-done.grads = bf16[16,104,256]{2,1,0:T(8,128)(2,1)S(1)} async-done(((bf16[16,104,256]{2,1,0:T(8,128)(2,1)}), bf16[16,104,256]{2,1,0:T(8,128)(2,1)S(1)}, u32[]{:S(2)}, u32[]{:S(2)}) %all-to-all-start) | async-done | bytes 852000 | tf_op jit(solution)/shard_map/all_to_all | solution.py:266
  32.7 0.0 copy-start.3
  32.7 0.0 copy-start.4
  32.7 4.5 %shard_map.86 = s16[16,32,128]{2,1,0:T(8,128)(2,1)} custom-call(bf16[14,3,16,1536]{3,2,1,0:T(8,128)(2,1)S(1)} %get-tuple-element.7.pat_early, bf16[14,3,16,2560]{3,2,1,0:T(8,128)(2,1)} %copy-done, bf16[16,104,256]{2,1,0:T(8,128)(2,1)S(1)} %all-to-all-done.grads), custom_call_target="tpu_custom_call" | custom-call | tf_op jit(solution)/shard_map/pallas_call | solution.py:284
  37.1 6.7 %all-to-all-start.1 = ((s16[16,32,128]{2,1,0:T(8,128)(2,1)}), s16[16,32,128]{2,1,0:T(8,128)(2,1)S(1)}, u32[]{:S(2)}, u32[]{:S(2)}) async-start(s16[16,32,128]{2,1,0:T(8,128)(2,1)} %shard_map.86), calls=%async_computation.1 | async-start | bytes 262144 | tf_op jit(solution)/shard_map/all_to_all | solution.py:299
  43.9 8.2 %all-to-all-done.1.parts = s16[16,32,128]{2,1,0:T(8,128)(2,1)S(1)} async-done(((s16[16,32,128]{2,1,0:T(8,128)(2,1)}), s16[16,32,128]{2,1,0:T(8,128)(2,1)S(1)}, u32[]{:S(2)}, u32[]{:S(2)}) %all-to-all-start.1) | async-done | bytes 131104 | tf_op jit(solution)/shard_map/all_to_all | solution.py:299
  52.1 0.6 shard_map.87
  52.8 21.8 %all_to_all.20.pieces = s16[32,16,128]{2,1,0:T(8,128)(2,1)S(1)} all-to-all(s16[32,16,128]{2,1,0:T(8,128)(2,1)S(1)} %get-tuple-element.9), channel_id=1, replica_groups=mesh['dp'=32,'aug'=16] {'dp'}, dimensions={0} | all-to-all | bytes 262144 | tf_op jit(solution)/shard_map/all_to_all | solution.py:312
  74.5 0.8 shard_map.88
  75.3 3.9 %all-to-all-start.3 = ((s16[32,16,128]{2,1,0:T(8,128)(2,1)}), s16[32,16,128]{2,1,0:T(8,128)(2,1)S(1)}, u32[]{:S(2)}, u32[]{:S(2)}) async-start(s16[32,16,128]{2,1,0:T(8,128)(2,1)} %shard_map.88), calls=%async_computation.3 | async-start | bytes 262144 | tf_op jit(solution)/shard_map/all_to_all | solution.py:320
  79.2 0.5 slice.7
  79.7 10.0 %all-to-all-done.3.chunks = s16[32,16,128]{2,1,0:T(8,128)(2,1)S(1)} async-done(((s16[32,16,128]{2,1,0:T(8,128)(2,1)}), s16[32,16,128]{2,1,0:T(8,128)(2,1)S(1)}, u32[]{:S(2)}, u32[]{:S(2)}) %all-to-all-start.3) | async-done | bytes 131104 | tf_op jit(solution)/shard_map/all_to_all | solution.py:320
  89.7 0.1 shard_map.89
  89.8 0.0 copy-done.3
  89.8 0.0 copy-done.4
  89.8 0.8 slice_multiply_fusion
Async XLA Ops:
  2.9 29.8 %all-to-all-start = ((bf16[16,104,256]{2,1,0:T(8,128)(2,1)}), bf16[16,104,256]{2,1,0:T(8,128)(2,1)S(1)}, u32[]{:S(2)}, u32[]{:S(2)}) async-start(bf16[16,104,256]{2,1,0:T(8,128)(2,1)} %bitcast.6), calls=%async_computation | async-start | bytes 1703936 | tf_op jit(solution)/shard_map/all_to_all | solution.py:266
  12.9 1.0 %copy-start.1 = (bf16[1,3,256,256]{3,2,1,0:T(8,128)(2,1)S(1)}, bf16[1,3,256,256]{3,2,1,0:T(8,128)(2,1)}, u32[]{:S(2)}) copy-start(bf16[1,3,256,256]{3,2,1,0:T(8,128)(2,1)} %param.6) | copy-start | bytes 1179652
  13.9 0.7 copy-start.2
  22.9 1.7 %copy-start = (bf16[14,3,16,2560]{3,2,1,0:T(8,128)(2,1)}, bf16[14,3,16,2560]{3,2,1,0:T(8,128)(2,1)S(1)}, u32[]{:S(2)}) copy-start(bf16[14,3,16,2560]{3,2,1,0:T(8,128)(2,1)S(1)} %get-tuple-element.8.pat_late) | copy-start | bytes 10321924
  32.7 57.1 %copy-start.3 = (f32[61152]{0:T(1024)S(1)}, f32[61152]{0:T(1024)}, u32[]{:S(2)}) copy-start(f32[61152]{0:T(1024)} %param.10) | copy-start | bytes 733828
  32.7 57.1 %copy-start.4 = (f32[61152]{0:T(1024)S(1)}, f32[61152]{0:T(1024)}, u32[]{:S(2)}) copy-start(f32[61152]{0:T(1024)} %param.11) | copy-start | bytes 733828
  37.1 15.0 %all-to-all-start.1 = ((s16[16,32,128]{2,1,0:T(8,128)(2,1)}), s16[16,32,128]{2,1,0:T(8,128)(2,1)S(1)}, u32[]{:S(2)}, u32[]{:S(2)}) async-start(s16[16,32,128]{2,1,0:T(8,128)(2,1)} %shard_map.86), calls=%async_computation.1 | async-start | bytes 262144 | tf_op jit(solution)/shard_map/all_to_all | solution.py:299
  75.3 14.4 %all-to-all-start.3 = ((s16[32,16,128]{2,1,0:T(8,128)(2,1)}), s16[32,16,128]{2,1,0:T(8,128)(2,1)S(1)}, u32[]{:S(2)}, u32[]{:S(2)}) async-start(s16[32,16,128]{2,1,0:T(8,128)(2,1)} %shard_map.88), calls=%async_computation.3 | async-start | bytes 262144 | tf_op jit(solution)/shard_map/all_to_all | solution.py:320

commit v7 on v5

--- a/solution.py
+++ b/solution.py
@@ -32,6 +32,7 @@
 SPARE = 8
 MIB = 1024 * 1024
 EARLY = 6
+LATE = (GRID - EARLY) // 2
 ORDER = list(range(0, AUG, 2)) + list(range(1, AUG, 2))
 PITCH = SIDE + SPARE
 
@@ -92,33 +93,49 @@
                 pat[v, c, :, place] = pair[h]
         return carry
 
-    for pat, begin, count in ((pat_early, 0, EARLY), (pat_late, EARLY, GRID - EARLY)):
+    pieces = [(pat_early, 0, EARLY)]
+    pieces += [(pat_late.at[part], EARLY + part * LATE, LATE) for part in range(2)]
+    for pat, begin, count in pieces:
         lax.fori_loop(0, CH * count, functools.partial(assemble, pat, begin, count), 0)
 
 
-def gradient_kernel(pat_early, pat_late, grads, msg, near, gord, flat, strip, sem):
-    fetch = pltpu.make_async_copy(pat_late, near, sem)
-    fetch.start()
-    flat[...] = jnp.zeros(flat.shape, jnp.float32)
-    for k in range(AUG):
+def gradient_kernel(
+    pat_early, pat_late, grads, msg, near, gord, flat, strip, total, sems
+):
+    late = LATE * SIDE
+    for part in range(2):
+        pltpu.make_async_copy(pat_late.at[part], near.at[part], sems.at[part]).start()
+
+    def turn(k):
         turned = grads[k].T
         for y in range(GRID):
-            gord[(y * AUG + k) * 16:(y * AUG + k + 1) * 16, :] = turned[y * 16:(y + 1) * 16, :]
-    total = jnp.dot(
+            place = pl.ds(pl.multiple_of(y * AUG * 16 + k * 16, 16), 16)
+            gord[place, :] = turned[y * 16:(y + 1) * 16, :]
+
+    flat[PATCH:, :] = jnp.zeros((12, LANES), jnp.float32)
+    for k in range(AUG):
+        turn(k)
+    total[:, 0:COLS] = jnp.dot(
         pat_early[...].reshape(PS * CH * 16, EARLY * SIDE),
         gord[0:EARLY * SIDE, :],
         preferred_element_type=jnp.float32,
     )
-    fetch.wait()
-    total = total + jnp.dot(
-        near[...].reshape(PS * CH * 16, (GRID - EARLY) * SIDE),
-        gord[EARLY * SIDE:, :],
-        preferred_element_type=jnp.float32,
-    )
+
+    def add_part(part, carry):
+        pltpu.make_async_copy(pat_late.at[part], near.at[part], sems.at[part]).wait()
+        rows = pl.ds(pl.multiple_of(EARLY * SIDE + part * late, 16), late)
+        total[:, 0:COLS] = total[:, 0:COLS] + jnp.dot(
+            near[part].reshape(PS * CH * 16, late),
+            gord[rows, :],
+            preferred_element_type=jnp.float32,
+        )
+        return carry
+
+    lax.fori_loop(0, 2, add_part, 0)
     for v in range(PS):
         for c in range(CH):
             first = v * CH * 16 + c * 16
-            flat[pl.ds(c * PS * PS + v, PS, stride=PS), 0:COLS] = total[first:first + PS, :]
+            flat[pl.ds(c * PS * PS + v, PS, stride=PS), 0:COLS] = total[first:first + PS, 0:COLS]
 
     values = flat[:, 0:COLS]
     squares = jnp.full((1, LANES), jnp.sum(values * values), jnp.float32)
@@ -245,7 +262,7 @@
         patch_kernel,
         out_shape=(
             jax.ShapeDtypeStruct((PS, CH, 16, EARLY * SIDE), jnp.bfloat16),
-            jax.ShapeDtypeStruct((PS, CH, 16, (GRID - EARLY) * SIDE), jnp.bfloat16),
+            jax.ShapeDtypeStruct((2, PS, CH, 16, LATE * SIDE), jnp.bfloat16),
         ),
         in_specs=[SMEM, SMEM, VMEM],
         out_specs=(VMEM, VMEM),
@@ -264,11 +281,12 @@
         in_specs=[VMEM, pl.BlockSpec(memory_space=pl.ANY), VMEM],
         out_specs=VMEM,
         scratch_shapes=[
-            pltpu.VMEM((PS, CH, 16, (GRID - EARLY) * SIDE), jnp.bfloat16),
+            pltpu.VMEM((2, PS, CH, 16, LATE * SIDE), jnp.bfloat16),
             pltpu.VMEM((AUG * SIDE, COLS), jnp.bfloat16),
             pltpu.VMEM((PATCH + 12, LANES), jnp.float32),
             pltpu.VMEM((MROWS, LANES), jnp.float32),
-            pltpu.SemaphoreType.DMA,
+            pltpu.VMEM((PS * CH * 16, LANES), jnp.float32),
+            pltpu.SemaphoreType.DMA((2,)),
         ],
         compiler_params=pltpu.CompilerParams(vmem_limit_bytes=48 * MIB),
     )(pat_early, pat_late, blocks)

time: 91.6 us -> 90.7 us (level)
  no operation moved by 1% of the time
where the time goes in v7:
time: 90.7 us; the launch traced here: 90.3 us
  waiting for transfers between devices  26.2 us (29%)
  blocking collectives  21.8 us (24%)
  starting transfers between devices  19.8 us (22%)
  Pallas kernels  14 us (15%)
  local copies, waits for them, and re-layouts  6.89 us (8%)
    all_to_all x1, blocking collectives, per_device(): pieces = lax.all_to_all(term, 'dp', 0, 0)  21.8 us
    all_to_all x1, waiting for transfers between devices, per_device(): gathered = lax.all_to_all(spread, 'dp', 0, 0)  10 us
    all_to_all x1, starting transfers between devices, per_device(): blocks = lax.all_to_all(blocks, 'aug', 0, 0)  9.24 us
    pallas_call x1, Pallas kernels, per_device(): pl.pallas_call(patch_kernel, out_shape=(jax.ShapeDtypeStruct((PS, CH, 16,...  8.42 us
    all_to_all x1, waiting for transfers between devices, per_device(): parts = lax.all_to_all(parts, 'aug', 0, 0, axis_index_groups=[ORDER])  8.22 us
    all_to_all x1, waiting for transfers between devices, per_device(): blocks = lax.all_to_all(blocks, 'aug', 0, 0)  7.99 us
    all_to_all x1, starting transfers between devices, per_device(): parts = lax.all_to_all(parts, 'aug', 0, 0, axis_index_groups=[ORDER])  6.75 us
    pallas_call x1, Pallas kernels, per_device(): pl.pallas_call(gradient_kernel, out_shape=jax.ShapeDtypeStruct((AUG, MROW...  4.09 us
  transfers between devices with their start and end apart: 3, of which 3 were waited for; matrix products, arithmetic and copies ran while one was open for 1% of the time, Pallas kernels for 9%

profile of v7, /device:TPU:8, one launch (start us, length us, event | category | flops | bytes accessed | tf_op | source)
XLA Modules:
  0.0 90.3 jit_solution(16752307404307450415)
XLA Ops:
  0.6 2.2 %copy.10 = bf16[1664,256]{1,0:T(8,128)(2,1)} copy(bf16[1664,256]{0,1:T(8,128)(2,1)} %bitcast.13) | data formatting | bytes 1703936 | tf_op jit(solution)/shard_map/transpose | solution.py:259
  2.9 9.2 %all-to-all-start = ((bf16[16,104,256]{2,1,0:T(8,128)(2,1)}), bf16[16,104,256]{2,1,0:T(8,128)(2,1)S(1)}, u32[]{:S(2)}, u32[]{:S(2)}) async-start(bf16[16,104,256]{2,1,0:T(8,128)(2,1)} %bitcast.6), calls=%async_computation | async-start | bytes 1703936 | tf_op jit(solution)/shard_map/all_to_all | solution.py:260
  12.1 0.8 copy.9.offs
  12.9 0.0 copy-start.1
  12.9 1.0 %copy-done.1 = bf16[1,3,256,256]{3,2,1,0:T(8,128)(2,1)S(1)} copy-done((bf16[1,3,256,256]{3,2,1,0:T(8,128)(2,1)S(1)}, bf16[1,3,256,256]{3,2,1,0:T(8,128)(2,1)}, u32[]{:S(2)}) %copy-start.1) | copy-done | bytes 393240
  13.9 0.0 copy-start.2
  13.9 0.7 copy-done.2
  14.5 8.4 %shard_map.85 = (bf16[14,3,16,1536]{3,2,1,0:T(8,128)(2,1)S(1)}, bf16[2,14,3,16,1280]{4,3,2,1,0:T(8,128)(2,1)S(1)}) custom-call(s32[16,2]{1,0:T(8,128)S(1)} %copy.9.offs, s32[16]{0:T(128)S(1)} %bitcast.12, bf16[3,256,256]{2,1,0:T(8,128)(2,1)S(1)} %bitcast.11), custom_call_target="tpu_custom_call" | custom-call | flops 20000000000 | bytes 20000000 | tf_op jit(solution)/shard_map/pallas_call | solution.py:261
  22.9 0.0 copy-start
  23.0 1.7 %copy-done = bf16[2,14,3,16,1280]{4,3,2,1,0:T(8,128)(2,1)} copy-done((bf16[2,14,3,16,1280]{4,3,2,1,0:T(8,128)(2,1)}, bf16[2,14,3,16,1280]{4,3,2,1,0:T(8,128)(2,1)S(1)}, u32[]{:S(2)}) %copy-start) | copy-done | bytes 3440664
  24.7 8.0 %all-to-all-done.grads = bf16[16,104,256]{2,1,0:T(8,128)(2,1)S(1)} async-done(((bf16[16,104,256]{2,1,0:T(8,128)(2,1)}), bf16[16,104,256]{2,1,0:T(8,128)(2,1)S(1)}, u32[]{:S(2)}, u32[]{:S(2)}) %all-to-all-start) | async-done | bytes 852000 | tf_op jit(solution)/shard_map/all_to_all | solution.py:260
  32.7 0.0 copy-start.3
  32.7 0.0 copy-start.4
  32.7 4.1 %shard_map.86 = s16[16,32,128]{2,1,0:T(8,128)(2,1)} custom-call(bf16[14,3,16,1536]{3,2,1,0:T(8,128)(2,1)S(1)} %get-tuple-element.7.pat_early, bf16[2,14,3,16,1280]{4,3,2,1,0:T(8,128)(2,1)} %copy-done, bf16[16,104,256]{2,1,0:T(8,128)(2,1)S(1)} %all-to-all-done.grads), custom_call_target="tpu_custom_call" | custom-call | tf_op jit(solution)/shard_map/pallas_call | solution.py:278
  36.8 6.7 %all-to-all-start.1 = ((s16[16,32,128]{2,1,0:T(8,128)(2,1)}), s16[16,32,128]{2,1,0:T(8,128)(2,1)S(1)}, u32[]{:S(2)}, u32[]{:S(2)}) async-start(s16[16,32,128]{2,1,0:T(8,128)(2,1)} %shard_map.86), calls=%async_computation.1 | async-start | bytes 262144 | tf_op jit(solution)/shard_map/all_to_all | solution.py:293
  43.5 8.2 %all-to-all-done.1.parts = s16[16,32,128]{2,1,0:T(8,128)(2,1)S(1)} async-done(((s16[16,32,128]{2,1,0:T(8,128)(2,1)}), s16[16,32,128]{2,1,0:T(8,128)(2,1)S(1)}, u32[]{:S(2)}, u32[]{:S(2)}) %all-to-all-start.1) | async-done | bytes 131104 | tf_op jit(solution)/shard_map/all_to_all | solution.py:293
  51.7 0.6 shard_map.87
  52.4 21.8 %all_to_all.20.pieces = s16[32,16,128]{2,1,0:T(8,128)(2,1)S(1)} all-to-all(s16[32,16,128]{2,1,0:T(8,128)(2,1)S(1)} %get-tuple-element.9), channel_id=1, replica_groups=mesh['dp'=32,'aug'=16] {'dp'}, dimensions={0} | all-to-all | bytes 262144 | tf_op jit(solution)/shard_map/all_to_all | solution.py:306
  74.2 0.8 shard_map.88
  74.9 3.9 %all-to-all-start.3 = ((s16[32,16,128]{2,1,0:T(8,128)(2,1)}), s16[32,16,128]{2,1,0:T(8,128)(2,1)S(1)}, u32[]{:S(2)}, u32[]{:S(2)}) async-start(s16[32,16,128]{2,1,0:T(8,128)(2,1)} %shard_map.88), calls=%async_computation.3 | async-start | bytes 262144 | tf_op jit(solution)/shard_map/all_to_all | solution.py:314
  78.8 0.5 slice.7
  79.3 10.0 %all-to-all-done.3.chunks = s16[32,16,128]{2,1,0:T(8,128)(2,1)S(1)} async-done(((s16[32,16,128]{2,1,0:T(8,128)(2,1)}), s16[32,16,128]{2,1,0:T(8,128)(2,1)S(1)}, u32[]{:S(2)}, u32[]{:S(2)}) %all-to-all-start.3) | async-done | bytes 131104 | tf_op jit(solution)/shard_map/all_to_all | solution.py:314
  89.4 0.1 shard_map.89
  89.4 0.0 copy-done.3
  89.4 0.0 copy-done.4
  89.4 0.8 slice_multiply_fusion
Async XLA Ops:
  2.9 29.8 %all-to-all-start = ((bf16[16,104,256]{2,1,0:T(8,128)(2,1)}), bf16[16,104,256]{2,1,0:T(8,128)(2,1)S(1)}, u32[]{:S(2)}, u32[]{:S(2)}) async-start(bf16[16,104,256]{2,1,0:T(8,128)(2,1)} %bitcast.6), calls=%async_computation | async-start | bytes 1703936 | tf_op jit(solution)/shard_map/all_to_all | solution.py:260
  12.9 1.0 %copy-start.1 = (bf16[1,3,256,256]{3,2,1,0:T(8,128)(2,1)S(1)}, bf16[1,3,256,256]{3,2,1,0:T(8,128)(2,1)}, u32[]{:S(2)}) copy-start(bf16[1,3,256,256]{3,2,1,0:T(8,128)(2,1)} %param.6) | copy-start | bytes 1179652
  13.9 0.7 copy-start.2
  22.9 1.7 %copy-start = (bf16[2,14,3,16,1280]{4,3,2,1,0:T(8,128)(2,1)}, bf16[2,14,3,16,1280]{4,3,2,1,0:T(8,128)(2,1)S(1)}, u32[]{:S(2)}) copy-start(bf16[2,14,3,16,1280]{4,3,2,1,0:T(8,128)(2,1)S(1)} %get-tuple-element.8.pat_late) | copy-start | bytes 10321924
  32.7 56.8 %copy-start.3 = (f32[61152]{0:T(1024)S(1)}, f32[61152]{0:T(1024)}, u32[]{:S(2)}) copy-start(f32[61152]{0:T(1024)} %param.10) | copy-start | bytes 733828
  32.7 56.8 %copy-start.4 = (f32[61152]{0:T(1024)S(1)}, f32[61152]{0:T(1024)}, u32[]{:S(2)}) copy-start(f32[61152]{0:T(1024)} %param.11) | copy-start | bytes 733828
  36.8 15.0 %all-to-all-start.1 = ((s16[16,32,128]{2,1,0:T(8,128)(2,1)}), s16[16,32,128]{2,1,0:T(8,128)(2,1)S(1)}, u32[]{:S(2)}, u32[]{:S(2)}) async-start(s16[16,32,128]{2,1,0:T(8,128)(2,1)} %shard_map.86), calls=%async_computation.1 | async-start | bytes 262144 | tf_op jit(solution)/shard_map/all_to_all | solution.py:293
  74.9 14.4 %all-to-all-start.3 = ((s16[32,16,128]{2,1,0:T(8,128)(2,1)}), s16[32,16,128]{2,1,0:T(8,128)(2,1)S(1)}, u32[]{:S(2)}, u32[]{:S(2)}) async-start(s16[32,16,128]{2,1,0:T(8,128)(2,1)} %shard_map.88), calls=%async_computation.3 | async-start | bytes 262144 | tf_op jit(solution)/shard_map/all_to_all | solution.py:314

commit v8 on v7

--- a/solution.py
+++ b/solution.py
@@ -107,7 +107,7 @@
         pltpu.make_async_copy(pat_late.at[part], near.at[part], sems.at[part]).start()
 
     def turn(k):
-        turned = grads[k].T
+        turned = grads[ORDER.index(k)].T
         for y in range(GRID):
             place = pl.ds(pl.multiple_of(y * AUG * 16 + k * 16, 16), 16)
             gord[place, :] = turned[y * 16:(y + 1) * 16, :]
@@ -192,7 +192,7 @@
     squares = jnp.zeros((1, 1), jnp.float32)
     opened = []
     for a in range(AUG):
-        part = plain(parts[ORDER.index(a)])
+        part = plain(parts[a])
         over = unpacked(part)
         step = step_of(over[6:7])
         opened.append(jnp.concatenate([part * step, over * step])[0:SROWS])
@@ -257,7 +257,7 @@
     aug_index = lax.axis_index("aug")
     images_in_all = lax.axis_size("dp")
     blocks = out_grads[0, 0].T.reshape(AUG, COLS, GRID * GRID)
-    blocks = lax.all_to_all(blocks, "aug", 0, 0)
+    blocks = lax.all_to_all(blocks, "aug", 0, 0, axis_index_groups=[ORDER])
     pat_early, pat_late = pl.pallas_call(
         patch_kernel,
         out_shape=(

time: 90.7 us -> 90.8 us (level)
  waiting for transfers between devices: 26.2 us -> 28.6 us
  starting transfers between devices: 19.8 us -> 17.5 us
    all_to_all x1, waiting for transfers between devices: 7.99 us -> 10.4 us  [per_device(): blocks = lax.all_to_all(blocks, 'aug', 0, 0, axis_index_groups=[ORDER])]
    all_to_all x1, starting transfers between devices: 6.75 us -> 4.39 us  [per_device(): parts = lax.all_to_all(parts, 'aug', 0, 0, axis_index_groups=[ORDER])]
where the time goes in v8:
time: 90.8 us; the launch traced here: 90.3 us
  waiting for transfers between devices  28.6 us (31%)
  blocking collectives  21.8 us (24%)
  starting transfers between devices  17.5 us (19%)
  Pallas kernels  14 us (15%)
  local copies, waits for them, and re-layouts  6.89 us (8%)
    all_to_all x1, blocking collectives, per_device(): pieces = lax.all_to_all(term, 'dp', 0, 0)  21.8 us
    all_to_all x1, waiting for transfers between devices, per_device(): blocks = lax.all_to_all(blocks, 'aug', 0, 0, axis_index_groups=[ORDER])  10.4 us
    all_to_all x1, waiting for transfers between devices, per_device(): gathered = lax.all_to_all(spread, 'dp', 0, 0)  10 us
    all_to_all x1, starting transfers between devices, per_device(): blocks = lax.all_to_all(blocks, 'aug', 0, 0, axis_index_groups=[ORDER])  9.23 us
    pallas_call x1, Pallas kernels, per_device(): pl.pallas_call(patch_kernel, out_shape=(jax.ShapeDtypeStruct((PS, CH, 16,...  8.43 us
    all_to_all x1, waiting for transfers between devices, per_device(): parts = lax.all_to_all(parts, 'aug', 0, 0, axis_index_groups=[ORDER])  8.22 us
    all_to_all x1, starting transfers between devices, per_device(): parts = lax.all_to_all(parts, 'aug', 0, 0, axis_index_groups=[ORDER])  4.39 us
    pallas_call x1, Pallas kernels, per_device(): pl.pallas_call(gradient_kernel, out_shape=jax.ShapeDtypeStruct((AUG, MROW...  4.09 us
  transfers between devices with their start and end apart: 3, of which 3 were waited for; matrix products, arithmetic and copies ran while one was open for 1% of the time, Pallas kernels for 9%

profile of v8, /device:TPU:8, one launch (start us, length us, event | category | flops | bytes accessed | tf_op | source)
XLA Modules:
  0.0 90.3 jit_solution(13041525577137787801)
XLA Ops:
  0.6 2.2 %copy.10 = bf16[1664,256]{1,0:T(8,128)(2,1)} copy(bf16[1664,256]{0,1:T(8,128)(2,1)} %bitcast.13) | data formatting | bytes 1703936 | tf_op jit(solution)/shard_map/transpose | solution.py:259
  2.9 9.2 %all-to-all-start = ((bf16[16,104,256]{2,1,0:T(8,128)(2,1)}), bf16[16,104,256]{2,1,0:T(8,128)(2,1)S(1)}, u32[]{:S(2)}, u32[]{:S(2)}) async-start(bf16[16,104,256]{2,1,0:T(8,128)(2,1)} %bitcast.6), calls=%async_computation | async-start | bytes 1703936 | tf_op jit(solution)/shard_map/all_to_all | solution.py:260
  12.1 0.8 copy.9.offs
  12.9 0.0 copy-start.1
  12.9 1.0 %copy-done.1 = bf16[1,3,256,256]{3,2,1,0:T(8,128)(2,1)S(1)} copy-done((bf16[1,3,256,256]{3,2,1,0:T(8,128)(2,1)S(1)}, bf16[1,3,256,256]{3,2,1,0:T(8,128)(2,1)}, u32[]{:S(2)}) %copy-start.1) | copy-done | bytes 393240
  13.9 0.0 copy-start.2
  13.9 0.7 copy-done.2
  14.5 8.4 %shard_map.85 = (bf16[14,3,16,1536]{3,2,1,0:T(8,128)(2,1)S(1)}, bf16[2,14,3,16,1280]{4,3,2,1,0:T(8,128)(2,1)S(1)}) custom-call(s32[16,2]{1,0:T(8,128)S(1)} %copy.9.offs, s32[16]{0:T(128)S(1)} %bitcast.12, bf16[3,256,256]{2,1,0:T(8,128)(2,1)S(1)} %bitcast.11), custom_call_target="tpu_custom_call" | custom-call | flops 20000000000 | bytes 20000000 | tf_op jit(solution)/shard_map/pallas_call | solution.py:261
  23.0 0.0 copy-start
  23.0 1.7 %copy-done = bf16[2,14,3,16,1280]{4,3,2,1,0:T(8,128)(2,1)} copy-done((bf16[2,14,3,16,1280]{4,3,2,1,0:T(8,128)(2,1)}, bf16[2,14,3,16,1280]{4,3,2,1,0:T(8,128)(2,1)S(1)}, u32[]{:S(2)}) %copy-start) | copy-done | bytes 3440664
  24.7 10.4 %all-to-all-done.grads = bf16[16,104,256]{2,1,0:T(8,128)(2,1)S(1)} async-done(((bf16[16,104,256]{2,1,0:T(8,128)(2,1)}), bf16[16,104,256]{2,1,0:T(8,128)(2,1)S(1)}, u32[]{:S(2)}, u32[]{:S(2)}) %all-to-all-start) | async-done | bytes 852000 | tf_op jit(solution)/shard_map/all_to_all | solution.py:260
  35.1 0.0 copy-start.3
  35.1 0.0 copy-start.4
  35.1 4.1 %shard_map.86 = s16[16,32,128]{2,1,0:T(8,128)(2,1)} custom-call(bf16[14,3,16,1536]{3,2,1,0:T(8,128)(2,1)S(1)} %get-tuple-element.7.pat_early, bf16[2,14,3,16,1280]{4,3,2,1,0:T(8,128)(2,1)} %copy-done, bf16[16,104,256]{2,1,0:T(8,128)(2,1)S(1)} %all-to-all-done.grads), custom_call_target="tpu_custom_call" | custom-call | tf_op jit(solution)/shard_map/pallas_call | solution.py:278
  39.2 4.4 %all-to-all-start.1 = ((s16[16,32,128]{2,1,0:T(8,128)(2,1)}), s16[16,32,128]{2,1,0:T(8,128)(2,1)S(1)}, u32[]{:S(2)}, u32[]{:S(2)}) async-start(s16[16,32,128]{2,1,0:T(8,128)(2,1)} %shard_map.86), calls=%async_computation.1 | async-start | bytes 262144 | tf_op jit(solution)/shard_map/all_to_all | solution.py:293
  43.6 8.2 %all-to-all-done.1.parts = s16[16,32,128]{2,1,0:T(8,128)(2,1)S(1)} async-done(((s16[16,32,128]{2,1,0:T(8,128)(2,1)}), s16[16,32,128]{2,1,0:T(8,128)(2,1)S(1)}, u32[]{:S(2)}, u32[]{:S(2)}) %all-to-all-start.1) | async-done | bytes 131104 | tf_op jit(solution)/shard_map/all_to_all | solution.py:293
  51.8 0.6 shard_map.87
  52.4 21.8 %all_to_all.20.pieces = s16[32,16,128]{2,1,0:T(8,128)(2,1)S(1)} all-to-all(s16[32,16,128]{2,1,0:T(8,128)(2,1)S(1)} %get-tuple-element.9), channel_id=1, replica_groups=mesh['dp'=32,'aug'=16] {'dp'}, dimensions={0} | all-to-all | bytes 262144 | tf_op jit(solution)/shard_map/all_to_all | solution.py:306
  74.2 0.8 shard_map.88
  75.0 3.9 %all-to-all-start.3 = ((s16[32,16,128]{2,1,0:T(8,128)(2,1)}), s16[32,16,128]{2,1,0:T(8,128)(2,1)S(1)}, u32[]{:S(2)}, u32[]{:S(2)}) async-start(s16[32,16,128]{2,1,0:T(8,128)(2,1)} %shard_map.88), calls=%async_computation.3 | async-start | bytes 262144 | tf_op jit(solution)/shard_map/all_to_all | solution.py:314
  78.9 0.5 slice.7
  79.4 10.0 %all-to-all-done.3.chunks = s16[32,16,128]{2,1,0:T(8,128)(2,1)S(1)} async-done(((s16[32,16,128]{2,1,0:T(8,128)(2,1)}), s16[32,16,128]{2,1,0:T(8,128)(2,1)S(1)}, u32[]{:S(2)}, u32[]{:S(2)}) %all-to-all-start.3) | async-done | bytes 131104 | tf_op jit(solution)/shard_map/all_to_all | solution.py:314
  89.4 0.1 shard_map.89
  89.5 0.0 copy-done.3
  89.5 0.0 copy-done.4
  89.5 0.8 slice_multiply_fusion
Async XLA Ops:
  2.9 32.2 %all-to-all-start = ((bf16[16,104,256]{2,1,0:T(8,128)(2,1)}), bf16[16,104,256]{2,1,0:T(8,128)(2,1)S(1)}, u32[]{:S(2)}, u32[]{:S(2)}) async-start(bf16[16,104,256]{2,1,0:T(8,128)(2,1)} %bitcast.6), calls=%async_computation | async-start | bytes 1703936 | tf_op jit(solution)/shard_map/all_to_all | solution.py:260
  12.9 1.0 %copy-start.1 = (bf16[1,3,256,256]{3,2,1,0:T(8,128)(2,1)S(1)}, bf16[1,3,256,256]{3,2,1,0:T(8,128)(2,1)}, u32[]{:S(2)}) copy-start(bf16[1,3,256,256]{3,2,1,0:T(8,128)(2,1)} %param.6) | copy-start | bytes 1179652
  13.9 0.7 copy-start.2
  23.0 1.7 %copy-start = (bf16[2,14,3,16,1280]{4,3,2,1,0:T(8,128)(2,1)}, bf16[2,14,3,16,1280]{4,3,2,1,0:T(8,128)(2,1)S(1)}, u32[]{:S(2)}) copy-start(bf16[2,14,3,16,1280]{4,3,2,1,0:T(8,128)(2,1)S(1)} %get-tuple-element.8.pat_late) | copy-start | bytes 10321924
  35.1 54.4 %copy-start.3 = (f32[61152]{0:T(1024)S(1)}, f32[61152]{0:T(1024)}, u32[]{:S(2)}) copy-start(f32[61152]{0:T(1024)} %param.10) | copy-start | bytes 733828
  35.1 54.4 %copy-start.4 = (f32[61152]{0:T(1024)S(1)}, f32[61152]{0:T(1024)}, u32[]{:S(2)}) copy-start(f32[61152]{0:T(1024)} %param.11) | copy-start | bytes 733828
  39.2 12.6 %all-to-all-start.1 = ((s16[16,32,128]{2,1,0:T(8,128)(2,1)}), s16[16,32,128]{2,1,0:T(8,128)(2,1)S(1)}, u32[]{:S(2)}, u32[]{:S(2)}) async-start(s16[16,32,128]{2,1,0:T(8,128)(2,1)} %shard_map.86), calls=%async_computation.1 | async-start | bytes 262144 | tf_op jit(solution)/shard_map/all_to_all | solution.py:293
  75.0 14.4 %all-to-all-start.3 = ((s16[32,16,128]{2,1,0:T(8,128)(2,1)}), s16[32,16,128]{2,1,0:T(8,128)(2,1)S(1)}, u32[]{:S(2)}, u32[]{:S(2)}) async-start(s16[32,16,128]{2,1,0:T(8,128)(2,1)} %shard_map.88), calls=%async_computation.3 | async-start | bytes 262144 | tf_op jit(solution)/shard_map/all_to_all | solution.py:314
